TPU v7x, 512 devices: a whole 4x4x16 slice. The times are simulated.
512 devices in a mesh: expert: 64 (over z, x), tensor: 8 (over y, core).
Axes of the slice: x: 4, y: 4, z: 16, core: 2. Of those that a mesh axis runs over, the one named last changes fastest.
Arguments:
- tokens: bfloat16 [8192, 2048], P(('expert', 'tensor')), may hold values from -40 to 40
- cotangent: bfloat16 [8192, 2048], P(('expert', 'tensor')), may hold values from -32 to 32
- gain: float32 [2048], replicated, may hold values from 0.1 to 1.9
- expert_ids: int32 [8192, 8], P('expert'), may hold values from 0 to 127, all different within a row; in each aligned block of 128 rows (0 to 127, 128 to 255, ...) at most 12 rows name the same one
- gate_probs: float32 [8192, 8], P('expert'), may hold values from 0.05 to 0.3
- gate_up_weight: bfloat16 [512, 2048, 384], P(('expert', 'tensor')), may hold values from -0.125 to 0.125
- down_weight: bfloat16 [512, 192, 2048], P(('expert', 'tensor')), may hold values from -0.21875 to 0.21875
Outputs:
- mixed: bfloat16 [8192, 2048], P(('expert', 'tensor'))
- token_grad: bfloat16 [8192, 2048], P(('expert', 'tensor'))
- prob_grad: float32 [8192, 8], P(('expert', 'tensor'))
- gain_grad: float32 [2048], replicated
- gate_up_grad: bfloat16 [512, 2048, 384], P(('expert', 'tensor'))
- down_grad: bfloat16 [512, 192, 2048], P(('expert', 'tensor'))
Inputs may be any that keep to these rules, and one draw needn't show every extreme that they name: `expert_ids`: in each aligned block of 128 rows, the tokens of one index of the expert axis, no expert is named by more than 12 rows.
All inputs are finite; a program needn't handle non-finite values.
Results may differ from a plain program's by a relative error of at most 0.009.
Values may be sent and summed in bfloat16 or wider, within the bound.
A program may use at most 128 MiB of HBM per device.

v0:
```python
import jax
import jax.numpy as jnp
from jax import lax
from jax.sharding import PartitionSpec as P

TOP = 8
EXP_DEV = 2


def normalize(rows):
    values = rows.astype(jnp.float32)
    inv_rms = lax.rsqrt(jnp.mean(values * values, axis=1, keepdims=True) + 1e-06)
    return (values * inv_rms, inv_rms)


def expert_forward(rows, gate_up, down_proj):
    projected = jnp.dot(rows, gate_up, preferred_element_type=jnp.float32)
    half_width = down_proj.shape[0]
    gate_pre = projected[:, :half_width]
    up_pre = projected[:, half_width:]
    sigmoid_gate = jax.nn.sigmoid(gate_pre)
    hidden = (gate_pre * sigmoid_gate * up_pre).astype(jnp.bfloat16)
    block_out = jnp.dot(hidden, down_proj, preferred_element_type=jnp.float32).astype(jnp.bfloat16)
    return (gate_pre, up_pre, sigmoid_gate, hidden, block_out)


def expert_backward(rows, slot_grads, gate_up, down_proj, gate_pre, up_pre, sigmoid_gate, hidden):
    hidden_grad = lax.dot_general(
        slot_grads, down_proj, (((1,), (1,)), ((), ())), preferred_element_type=jnp.float32
    )
    gate_grad = (
        hidden_grad * up_pre * sigmoid_gate * (1.0 + gate_pre * (1.0 - sigmoid_gate))
    ).astype(jnp.bfloat16)
    up_grad = (hidden_grad * gate_pre * sigmoid_gate).astype(jnp.bfloat16)
    joined_grad = jnp.concatenate([gate_grad, up_grad], axis=1)
    down_part = lax.dot_general(
        hidden, slot_grads, (((0,), (0,)), ((), ())), preferred_element_type=jnp.float32
    ).astype(jnp.bfloat16)
    gate_up_part = lax.dot_general(
        rows, joined_grad, (((0,), (0,)), ((), ())), preferred_element_type=jnp.float32
    ).astype(jnp.bfloat16)
    input_grad = lax.dot_general(
        joined_grad, gate_up, (((1,), (1,)), ((), ())), preferred_element_type=jnp.float32
    ).astype(jnp.bfloat16)
    return (input_grad, gate_up_part, down_part)


def shards(tokens, cotangent, gain, expert_ids, gate_probs, gate_up_weight, down_weight):
    tensor_size = lax.axis_size("tensor")
    expert_size = lax.axis_size("expert")
    my_rank = lax.axis_index("tensor")
    blocks_each = tensor_size // EXP_DEV
    my_type = my_rank // blocks_each
    group_rows = expert_ids.shape[0]
    features = tokens.shape[1]
    capacity = 3 * group_rows * TOP // (2 * EXP_DEV * expert_size)
    highest = lax.Precision.HIGHEST
    scaled_own, inv_own = normalize(tokens)
    carried = (scaled_own * gain[None, :]).astype(jnp.bfloat16)
    group_first, group_grads = (
        lax.all_gather(carried, "tensor", axis=0, tiled=True),
        lax.all_gather(cotangent, "tensor", axis=0, tiled=True),
    )
    targets = jnp.arange(expert_size, dtype=jnp.int32) * EXP_DEV + my_type
    matches = expert_ids[:, :, None] == targets[None, None, :]
    chosen = jnp.any(matches, axis=1)
    weight_of = jnp.sum(jnp.where(matches, gate_probs[:, :, None], 0.0), axis=1)
    slot_of = jnp.sum(
        jnp.where(matches, jnp.arange(TOP, dtype=jnp.int32)[None, :, None], 0), axis=1
    )
    row_ids = jnp.arange(group_rows, dtype=jnp.int32)
    earlier = (row_ids[None, :] < row_ids[:, None]).astype(jnp.bfloat16)
    rank_in = jnp.dot(
        earlier, chosen.astype(jnp.bfloat16), preferred_element_type=jnp.float32
    ).astype(jnp.int32)
    placed = chosen.T[:, None, :] & (
        rank_in.T[:, None, :] == jnp.arange(capacity, dtype=jnp.int32)[None, :, None]
    )
    source = jnp.sum(jnp.where(placed, row_ids[None, None, :], 0), axis=2)
    filled = jnp.any(placed, axis=2)
    slot_prob = jnp.sum(jnp.where(placed, weight_of.T[:, None, :], 0.0), axis=2)
    slot_index = jnp.sum(jnp.where(placed, slot_of.T[:, None, :], 0), axis=2)
    sent_rows = jnp.where(
        filled[:, :, None], jnp.take(group_first, source, axis=0), jnp.zeros((), jnp.bfloat16)
    )
    sent_grads = (
        slot_prob[:, :, None] * jnp.take(group_grads, source, axis=0).astype(jnp.float32)
    ).astype(jnp.bfloat16)
    gate_up = gate_up_weight[0]
    down_proj = down_weight[0]
    arrived_rows, arrived_grads = (
        lax.all_to_all(sent_rows, "expert", split_axis=0, concat_axis=0, tiled=True),
        lax.all_to_all(sent_grads, "expert", split_axis=0, concat_axis=0, tiled=True),
    )
    rows = arrived_rows.reshape(-1, features)
    slot_grads = arrived_grads.reshape(-1, features)
    gate_pre, up_pre, sigmoid_gate, hidden, block_out = expert_forward(rows, gate_up, down_proj)
    out_slots = block_out.reshape(expert_size, capacity, features)
    input_grad, gate_up_part, down_part = expert_backward(
        rows, slot_grads, gate_up, down_proj, gate_pre, up_pre, sigmoid_gate, hidden
    )
    input_slots = input_grad.reshape(expert_size, capacity, features)
    out_back, input_back = (
        lax.all_to_all(out_slots, "expert", split_axis=0, concat_axis=0, tiled=True),
        lax.all_to_all(input_slots, "expert", split_axis=0, concat_axis=0, tiled=True),
    )
    out_flat = out_back.reshape(-1, features)
    input_flat = input_back.reshape(-1, features)
    used_source = source.reshape(-1)
    used_filled = filled.reshape(-1)
    used_prob = slot_prob.reshape(-1)
    used_index = slot_index.reshape(-1)
    cot_slots = jnp.take(group_grads, used_source, axis=0)
    prob_values = jnp.einsum("sd,sd->s", cot_slots, out_flat, preferred_element_type=jnp.float32)
    hit = (row_ids[:, None] == used_source[None, :]) & used_filled[None, :]
    input_part = jnp.dot(hit.astype(jnp.bfloat16), input_flat, preferred_element_type=jnp.float32)
    weighting = jnp.where(hit, used_prob[None, :], 0.0)
    out_part = jnp.dot(
        weighting,
        out_flat.astype(jnp.float32),
        precision=highest,
        preferred_element_type=jnp.float32,
    )
    prob_columns = jnp.where(
        used_index[:, None] == jnp.arange(TOP, dtype=jnp.int32)[None, :], prob_values[:, None], 0.0
    )
    prob_part = jnp.dot(
        hit.astype(jnp.float32), prob_columns, precision=highest, preferred_element_type=jnp.float32
    )
    out_sum, normed_grad, prob_grad = (
        lax.psum_scatter(out_part, "tensor", scatter_dimension=0, tiled=True),
        lax.psum_scatter(input_part, "tensor", scatter_dimension=0, tiled=True),
        lax.psum_scatter(prob_part, "tensor", scatter_dimension=0, tiled=True),
    )
    mixed = (tokens.astype(jnp.float32) + out_sum).astype(jnp.bfloat16)
    gain_side = normed_grad * gain[None, :]
    token_grad = (
        cotangent.astype(jnp.float32)
        + inv_own
        * (gain_side - scaled_own * jnp.mean(gain_side * scaled_own, axis=1, keepdims=True))
    ).astype(jnp.bfloat16)
    gain_grad = lax.psum(jnp.sum(normed_grad * scaled_own, axis=0), ("expert", "tensor"))
    return (mixed, token_grad, prob_grad, gain_grad, gate_up_part[None], down_part[None])


def solution(mesh):
    in_specs = (
        P(("expert", "tensor"), None),
        P(("expert", "tensor"), None),
        P(),
        P("expert", None),
        P("expert", None),
        P(("expert", "tensor"), None, None),
        P(("expert", "tensor"), None, None),
    )
    out_specs = (
        P(("expert", "tensor"), None),
        P(("expert", "tensor"), None),
        P(("expert", "tensor"), None),
        P(),
        P(("expert", "tensor"), None, None),
        P(("expert", "tensor"), None, None),
    )
    return jax.shard_map(shards, mesh=mesh, in_specs=in_specs, out_specs=out_specs, check_vma=False)
```

profile of v0, /device:TPU:1, one launch (start us, length us, event | category | flops | bytes accessed | tf_op | source)
XLA Modules:
  0.0 1010.0 jit_solution(2385473956684537475)
XLA Ops:
  12.2 19.8 %all_gather.6 = bf16[128,2048]{1,0:T(8,128)(2,1)S(1)} all-gather(bf16[16,2048]{1,0:T(8,128)(2,1)S(1)} %fusion.37), channel_id=1, replica_groups=mesh['expert'=64,'tensor'=8] {'tensor'}, dimensions={0}, use_global_device_ids=true | all-gather | bytes 589824 | tf_op jit(solution)/shard_map/all_gather | solution.py:61
  32.1 4.3 gather_fusion.1
  36.3 6.1 reshape.141
  42.4 3.9 select_select_fusion
  46.3 13.8 %all-to-all-start = ((bf16[64,12,2048]{2,1,0:T(8,128)(2,1)}), bf16[64,12,2048]{2,1,0:T(8,128)(2,1)}, u32[]{:S(2)}, u32[]{:S(2)}) async-start(bf16[64,12,2048]{2,1,0:T(8,128)(2,1)} %select_select_fusion), calls=%async_computation | async-start | bytes 8388608 | tf_op jit(solution)/shard_map/all_to_all | solution.py:92
  60.5 13.4 %all_gather.7 = bf16[128,2048]{1,0:T(8,128)(2,1)S(1)} all-gather(bf16[16,2048]{1,0:T(8,128)(2,1)S(1)} %copy-done.4), channel_id=1, replica_groups=mesh['expert'=64,'tensor'=8] {'tensor'}, dimensions={0}, use_global_device_ids=true | all-gather | bytes 589824 | tf_op jit(solution)/shard_map/all_gather | solution.py:62
  73.9 4.3 gather_fusion.2
  78.2 6.1 reshape.145
  84.3 4.1 multiply_convert_fusion
  88.5 155.2 %all-to-all-done = bf16[64,12,2048]{2,1,0:T(8,128)(2,1)} async-done(((bf16[64,12,2048]{2,1,0:T(8,128)(2,1)}), bf16[64,12,2048]{2,1,0:T(8,128)(2,1)}, u32[]{:S(2)}, u32[]{:S(2)}) %all-to-all-start) | async-done | bytes 3145760 | tf_op jit(solution)/shard_map/all_to_all | solution.py:92
  243.6 12.1 %all-to-all-start.2 = ((bf16[64,12,2048]{2,1,0:T(8,128)(2,1)}), bf16[64,12,2048]{2,1,0:T(8,128)(2,1)}, u32[]{:S(2)}, u32[]{:S(2)}) async-start(bf16[64,12,2048]{2,1,0:T(8,128)(2,1)} %multiply_convert_fusion), calls=%async_computation.3 | async-start | bytes 8388608 | tf_op jit(solution)/shard_map/all_to_all | solution.py:93
  255.7 6.2 reshape.103
  261.9 4.3 fusion.4
  266.2 173.2 %all-to-all-done.2 = bf16[64,12,2048]{2,1,0:T(8,128)(2,1)} async-done(((bf16[64,12,2048]{2,1,0:T(8,128)(2,1)}), bf16[64,12,2048]{2,1,0:T(8,128)(2,1)}, u32[]{:S(2)}, u32[]{:S(2)}) %all-to-all-start.2) | async-done | bytes 3145760 | tf_op jit(solution)/shard_map/all_to_all | solution.py:93
  439.4 6.2 reshape.106
  445.6 4.3 multiply_convert_fusion.2
  452.6 6.1 reshape.104
  458.7 11.9 %all-to-all-start.1 = ((bf16[64,12,2048]{2,1,0:T(8,128)(2,1)}), bf16[64,12,2048]{2,1,0:T(8,128)(2,1)}, u32[]{:S(2)}, u32[]{:S(2)}) async-start(bf16[64,12,2048]{2,1,0:T(8,128)(2,1)} %reshape.104), calls=%async_computation.1 | async-start | bytes 8388608 | tf_op jit(solution)/shard_map/all_to_all | solution.py:104
  470.6 3.6 convolution_convert_fusion
  474.1 6.1 reshape.107
  480.2 173.7 %all-to-all-done.1 = bf16[64,12,2048]{2,1,0:T(8,128)(2,1)} async-done(((bf16[64,12,2048]{2,1,0:T(8,128)(2,1)}), bf16[64,12,2048]{2,1,0:T(8,128)(2,1)}, u32[]{:S(2)}, u32[]{:S(2)}) %all-to-all-start.1) | async-done | bytes 3145760 | tf_op jit(solution)/shard_map/all_to_all | solution.py:104
  654.0 11.9 %all-to-all-start.3 = ((bf16[64,12,2048]{2,1,0:T(8,128)(2,1)}), bf16[64,12,2048]{2,1,0:T(8,128)(2,1)}, u32[]{:S(2)}, u32[]{:S(2)}) async-start(bf16[64,12,2048]{2,1,0:T(8,128)(2,1)} %reshape.107), calls=%async_computation.4 | async-start | bytes 8388608 | tf_op jit(solution)/shard_map/all_to_all | solution.py:105
  666.6 4.3 gather_fusion
  670.9 6.2 reshape.105
  677.0 4.0 fusion
  682.3 167.0 %all-to-all-done.3 = bf16[64,12,2048]{2,1,0:T(8,128)(2,1)} async-done(((bf16[64,12,2048]{2,1,0:T(8,128)(2,1)}), bf16[64,12,2048]{2,1,0:T(8,128)(2,1)}, u32[]{:S(2)}, u32[]{:S(2)}) %all-to-all-start.3) | async-done | bytes 3145760 | tf_op jit(solution)/shard_map/all_to_all | solution.py:105
  849.3 6.2 reshape.108
  855.5 3.5 fusion.15
  859.1 4.3 fusion.11
  863.5 3.7 fusion.2
  871.6 23.3 %reduce-scatter.8.cloned.1.call-done = f32[16,2048]{1,0:T(8,128)} async-done(((f32[128,2048]{1,0:T(8,128)}), f32[16,2048]{1,0:T(8,128)}) %reduce-scatter.8.cloned.1.call-update) | async-done | bytes 131088 | tf_op jit(solution)/shard_map/reduce_scatter | solution.py:132
  896.0 105.8 %psum.7 = f32[2048]{0:T(1024)} all-reduce(f32[2048]{0:T(1024)S(1)} %get-tuple-element.7), channel_id=1, replica_groups=mesh['expert'=64,'tensor'=8] {'expert','tensor'}, use_global_device_ids=true, to_apply=%region_13.15 | all-reduce | flops 2048 | bytes 16384 | tf_op jit(solution)/shard_map/psum | solution.py:142
  (64 shorter events, 17.4 us)
Async XLA Ops:
  7.2 254.7 %copy-start = (bf16[1,2048,384]{2,1,0:T(8,128)(2,1)S(1)}, bf16[1,2048,384]{2,1,0:T(8,128)(2,1)}, u32[]{:S(2)}) copy-start(bf16[1,2048,384]{2,1,0:T(8,128)(2,1)} %param.14) | copy-start | bytes 4718596
  46.3 13.8 %copy-start.6 = (s32[128,8]{0,1:T(8,128)S(1)}, s32[128,8]{0,1:T(8,128)}, u32[]{:S(2)}) copy-start(s32[128,8]{0,1:T(8,128)} %param.12) | copy-start | bytes 12292
  46.3 13.9 %copy-start.7 = (f32[128,8]{0,1:T(8,128)S(1)}, f32[128,8]{0,1:T(8,128)}, u32[]{:S(2)}) copy-start(f32[128,8]{0,1:T(8,128)} %param.13) | copy-start | bytes 12292
  46.3 14.2 %copy-start.4 = (bf16[16,2048]{1,0:T(8,128)(2,1)S(1)}, bf16[16,2048]{1,0:T(8,128)(2,1)}, u32[]{:S(2)}) copy-start(bf16[16,2048]{1,0:T(8,128)(2,1)} %param.10) | copy-start | bytes 196612
  46.3 197.3 %all-to-all-start = ((bf16[64,12,2048]{2,1,0:T(8,128)(2,1)}), bf16[64,12,2048]{2,1,0:T(8,128)(2,1)}, u32[]{:S(2)}, u32[]{:S(2)}) async-start(bf16[64,12,2048]{2,1,0:T(8,128)(2,1)} %select_select_fusion), calls=%async_computation | async-start | bytes 8388608 | tf_op jit(solution)/shard_map/all_to_all | solution.py:92
  243.6 195.8 %all-to-all-start.2 = ((bf16[64,12,2048]{2,1,0:T(8,128)(2,1)}), bf16[64,12,2048]{2,1,0:T(8,128)(2,1)}, u32[]{:S(2)}, u32[]{:S(2)}) async-start(bf16[64,12,2048]{2,1,0:T(8,128)(2,1)} %multiply_convert_fusion), calls=%async_computation.3 | async-start | bytes 8388608 | tf_op jit(solution)/shard_map/all_to_all | solution.py:93
  266.2 179.4 %copy-start.3 = (bf16[1,192,2048]{2,1,0:T(8,128)(2,1)S(1)}, bf16[1,192,2048]{2,1,0:T(8,128)(2,1)}, u32[]{:S(2)}) copy-start(bf16[1,192,2048]{2,1,0:T(8,128)(2,1)} %param.15) | copy-start | bytes 2359300
  458.7 11.9 %copy-start.8 = (bf16[768,192]{0,1:T(8,128)(2,1)S(1)}, bf16[768,192]{0,1:T(8,128)(2,1)}, u32[]{:S(2)}) copy-start(bf16[768,192]{0,1:T(8,128)(2,1)} %get-tuple-element.11) | copy-start | bytes 884740
  458.7 11.9 %copy-start.9 = (bf16[768,192]{0,1:T(8,128)(2,1)S(1)}, bf16[768,192]{0,1:T(8,128)(2,1)}, u32[]{:S(2)}) copy-start(bf16[768,192]{0,1:T(8,128)(2,1)} %get-tuple-element.12) | copy-start | bytes 884740
  458.7 195.3 %all-to-all-start.1 = ((bf16[64,12,2048]{2,1,0:T(8,128)(2,1)}), bf16[64,12,2048]{2,1,0:T(8,128)(2,1)}, u32[]{:S(2)}, u32[]{:S(2)}) async-start(bf16[64,12,2048]{2,1,0:T(8,128)(2,1)} %reshape.104), calls=%async_computation.1 | async-start | bytes 8388608 | tf_op jit(solution)/shard_map/all_to_all | solution.py:104
  654.0 195.3 %all-to-all-start.3 = ((bf16[64,12,2048]{2,1,0:T(8,128)(2,1)}), bf16[64,12,2048]{2,1,0:T(8,128)(2,1)}, u32[]{:S(2)}, u32[]{:S(2)}) async-start(bf16[64,12,2048]{2,1,0:T(8,128)(2,1)} %reshape.107), calls=%async_computation.4 | async-start | bytes 8388608 | tf_op jit(solution)/shard_map/all_to_all | solution.py:105
  665.9 204.3 %reduce-scatter.10.cloned.1.call-start = ((), (), s32[]{:S(2)}) async-start(), calls=%async_computation.9 | async-start | bytes 73728
  682.2 212.6 %reduce-scatter.8.cloned.1.call-start = ((), (), s32[]{:S(2)}) async-start(), calls=%async_computation.8 | async-start | bytes 1179648 | tf_op jit(solution)/shard_map/reduce_scatter | solution.py:132
  858.9 142.8 %reduce-scatter.6.cloned.1.call-start = ((), (), s32[]{:S(2)}) async-start(), calls=%async_computation.7 | async-start | bytes 1179648 | tf_op jit(solution)/shard_map/reduce_scatter | solution.py:131
  863.4 3.7 copy-start.1
  867.2 27.7 %copy-start.2 = (bf16[16,2048]{1,0:T(8,128)(2,1)S(1)}, bf16[16,2048]{1,0:T(8,128)(2,1)}, u32[]{:S(2)}) copy-start(bf16[16,2048]{1,0:T(8,128)(2,1)} %param.9) | copy-start | bytes 196612
  867.2 27.7 %copy-start.5 = (f32[2048]{0:T(1024)S(1)}, f32[2048]{0:T(1024)}, u32[]{:S(2)}) copy-start(f32[2048]{0:T(1024)} %param.11) | copy-start | bytes 24580
Sparse Core Ops, SparseCore 0:
  682.4 38.4 reduce-scatter.9
  859.1 35.7 reduce-scatter.7
  897.9 38.6 reduce-scatter.5
where the time goes:
time: 1010 us
  waiting for transfers between devices  692 us (69%)
  blocking collectives  139 us (14%)
  local copies, waits for them, and re-layouts  64.5 us (6%)
  starting transfers between devices  49.8 us (5%)
  matrix products  30.7 us (3%)
  other arithmetic  19.6 us (2%)
  between operations  14 us (1%)
    all_to_all x1, waiting for transfers between devices, shards(): lax.all_to_all(out_slots, 'expert', split_axis=0, concat_axis=0, tiled=True)  174 us
    all_to_all x1, waiting for transfers between devices, shards(): lax.all_to_all(sent_grads, 'expert', split_axis=0, concat_axis=0, tiled=T...  173 us
    all_to_all x1, waiting for transfers between devices, shards(): lax.all_to_all(input_slots, 'expert', split_axis=0, concat_axis=0, tiled=...  167 us
    all_to_all x1, waiting for transfers between devices, shards(): lax.all_to_all(sent_rows, 'expert', split_axis=0, concat_axis=0, tiled=True)  155 us
    psum x1, blocking collectives, shards(): lax.psum(jnp.sum(normed_grad * scaled_own, axis=0), ('expert', 'tensor'))  106 us
    reduce_scatter x1, waiting for transfers between devices, shards(): lax.psum_scatter(input_part, 'tensor', scatter_dimension=0, tiled=True)  23.3 us
  transfers between devices with their start and end apart: 7, of which 5 were waited for; matrix products, arithmetic and copies ran while one was open for 7% of the time, Pallas kernels for 0%

commit v1 on v0

v1 whole, which is shorter than its diff:
```python
import functools

import jax
import jax.numpy as jnp
import numpy as np
from jax import lax
from jax.experimental import pallas as pl
from jax.experimental.pallas import tpu as pltpu
from jax.sharding import PartitionSpec as P

TOP = 8
NZ, NX, NY, NC = 16, 4, 4, 2
NT = NY * NC
TOK = 128
OWN = 16
CAP = 12
FEAT = 256
BATCH = 4
NB = NZ // BATCH
CHUNK = BATCH * CAP
ROWS = NX * CHUNK
SLOTS = NX * 2 * CHUNK
WIDE = BATCH * TOK
ORDER = [0, 1, -1, 2, -2, 3, -3, 4, -4, 5, -5, 6, -6, 7, -7, 8]
SLOT_OF = {d: s for s, d in enumerate(ORDER)}
SLOT_OF[-8] = SLOT_OF[8]
BF, F32 = jnp.bfloat16, jnp.float32


def place():
    e, t = lax.axis_index("expert"), lax.axis_index("tensor")
    return e, t, e // NX, lax.rem(e, NX), t // NC, lax.rem(t, NC)


def remote(src, dst, send, recv, device):
    return pltpu.make_async_remote_copy(
        src_ref=src, dst_ref=dst, send_sem=send, recv_sem=recv,
        device_id=device, device_id_type=pl.DeviceIdType.MESH,
    )


def greet(e, t, z, x):
    barrier = pltpu.get_barrier_semaphore()
    peers = [(e, lax.rem(t + i, NT)) for i in range(1, NT)]
    peers += [(z * NX + lax.rem(x + i, NX), t) for i in range(1, NX)]
    peers += [(lax.rem(z + i, NZ) * NX + x, t) for i in (1, NZ - 1)]
    for peer in peers:
        pl.semaphore_signal(barrier, inc=1, device_id=peer, device_id_type=pl.DeviceIdType.MESH)
    pl.semaphore_wait(barrier, len(peers))


def fill_select(codes, rmat, select):
    for f in range(2 * NX):
        hit = codes[f : f + 1, :] == rmat
        rows = pl.ds(f * CHUNK, CHUNK)
        select[0, rows, :] = jnp.where(hit, 1.0, 0.0).astype(BF)
        select[1, rows, :] = jnp.where(hit, codes[8 + f : 9 + f, :], 0.0).astype(BF)
        select[2, rows, :] = jnp.where(hit, codes[16 + f : 17 + f, :], 0.0).astype(BF)


def dispatch_kernel(
    own_ref, meta_ref, rmat_ref, tri_ref, rows_ref, codes_ref,
    zbuf, xs, yb, select,
    a_send, a_recv, z_send, z_recv, x_send, x_recv, y_send, y_recv, c_send, c_recv, local,
):
    e, t, z, x, y, c = place()
    phi = c * NY + y
    half = y // 2
    greet(e, t, z, x)
    started = []

    def feat(index):
        return pl.ds(pl.multiple_of(index * FEAT, FEAT), FEAT)

    stays = []
    for arr in range(2):
        row_at = pl.ds(pl.multiple_of(arr * TOK + t * OWN, OWN), OWN)
        for i in range(1, NT):
            other = lax.rem(t + i, NT)
            their = lax.rem(other, NC) * NY + other // NC
            n = arr * (NT - 1) + i - 1
            copy = remote(
                own_ref.at[arr, :, feat(their)], zbuf.at[0, row_at, :],
                a_send.at[n], a_recv.at[n], (e, other),
            )
            copy.start()
            started.append(copy)
        stay = pltpu.make_async_copy(own_ref.at[arr, :, feat(phi)], zbuf.at[0, row_at, :], local.at[arr])
        stay.start()
        stays.append(stay)
    zbuf[0, 2 * TOK :, :] = meta_ref[...]
    for copy in started:
        copy.wait_recv()
    for stay in stays:
        stay.wait()

    right = (lax.rem(z + 1, NZ) * NX + x, t)
    left = (lax.rem(z + NZ - 1, NZ) * NX + x, t)
    parts = (pl.ds(0, TOK), pl.ds(TOK, TOK + OWN))

    def hop(step, way):
        sign = -1 if way == 0 else 1
        src, dst = SLOT_OF[sign * (step - 1)], SLOT_OF[sign * step]
        copies = []
        for p, part in enumerate(parts):
            n = (way * 8 + step - 1) * 2 + p
            copy = remote(
                zbuf.at[src, part, :], zbuf.at[dst, part, :],
                z_send.at[n], z_recv.at[n], right if way == 0 else left,
            )
            copies.append(copy)
        return copies

    def stage_x(b):
        base = lax.convert_element_type(z * (2 * NX), F32)
        named = base + lax.broadcasted_iota(jnp.int32, (8, TOK), 0).astype(F32)
        chosen, high, low = [], [], []
        for j in range(BATCH):
            meta = zbuf[b * BATCH + j, 2 * TOK :, :].astype(F32)
            got, hi, lo = jnp.zeros((8, TOK), F32), jnp.zeros((8, TOK), F32), jnp.zeros((8, TOK), F32)
            for k in range(TOP):
                same = meta[k : k + 1, :TOK] == named
                got = got + jnp.where(same, 1.0, 0.0)
                hi = hi + jnp.where(same, meta[8 + k : 9 + k, :TOK], 0.0)
                lo = lo + jnp.where(same, meta[k : k + 1, TOK:], 0.0)
            chosen.append(got)
            high.append(hi)
            low.append(lo)
        taken = jnp.concatenate(chosen, axis=0)
        rank = jnp.dot(taken.astype(BF), tri_ref[...], preferred_element_type=F32)
        code = jnp.where(taken > 0.5, rank, -1.0)
        codes = jnp.concatenate(
            [
                jnp.concatenate([code[8 * j : 8 * j + 8] for j in range(BATCH)], axis=1),
                jnp.concatenate(high, axis=1),
                jnp.concatenate(low, axis=1),
            ],
            axis=0,
        )
        codes_ref[b] = codes
        fill_select(codes, rmat_ref[...], select)
        these = pl.ds(b * BATCH, BATCH)
        normed = zbuf[these, 0:TOK, :].reshape(WIDE, FEAT)
        cot = zbuf[these, TOK : 2 * TOK, :].reshape(WIDE, FEAT)
        picked = jnp.dot(select[0], normed, preferred_element_type=F32).astype(BF)
        grads = (
            jnp.dot(select[1], cot, preferred_element_type=F32)
            + jnp.dot(select[2], cot, preferred_element_type=F32)
        ).astype(BF)
        xs[b, :, :, 0] = picked.reshape(NX, 2, CHUNK, FEAT)
        xs[b, :, :, 1] = grads.reshape(NX, 2, CHUNK, FEAT)
        at = pl.ds(pl.multiple_of(x * CHUNK, 16), CHUNK)
        copies = []
        for i in range(1, NX):
            other = lax.rem(x + i, NX)
            n = b * (NX - 1) + i - 1
            copy = remote(
                xs.at[b, other], yb.at[b, :, :, at, :],
                x_send.at[n], x_recv.at[n], (z * NX + other, t),
            )
            copy.start()
            copies.append(copy)
        stay = pltpu.make_async_copy(xs.at[b, x], yb.at[b, :, :, at, :], local.at[2 + b])
        stay.start()
        return copies, stay

    def stage_y(b, earlier):
        copies, stay = earlier
        for copy in copies:
            copy.wait_recv()
        stay.wait()
        where = pl.ds(b * ROWS, ROWS)
        sent = []
        for i in range(1, NY):
            other = lax.rem(y + i, NY)
            n = b * (NY - 1) + i - 1
            copy = remote(
                yb.at[b, other // 2], rows_ref.at[:, where, feat(phi)],
                y_send.at[n], y_recv.at[n], (e, other * NC + c),
            )
            copy.start()
            sent.append(copy)
        keep = pltpu.make_async_copy(yb.at[b, half], rows_ref.at[:, where, feat(phi)], local.at[2 + NB + b])
        keep.start()
        return sent, keep

    def stage_c(b, earlier):
        sent, keep = earlier
        for copy in sent:
            copy.wait_recv()
        keep.wait()
        block = rows_ref.at[
            :, pl.ds(b * ROWS, ROWS), pl.ds(pl.multiple_of(c * (NY * FEAT), NY * FEAT), NY * FEAT)
        ]
        copy = remote(block, block, c_send.at[b], c_recv.at[b], (e, y * NC + 1 - c))
        copy.start()
        return copy

    flying = {}
    for way in range(2):
        flying[way] = hop(1, way)
        for copy in flying[way]:
            copy.start()
            started.append(copy)
    xdone, ydone, cdone = {}, {}, {}
    for step in range(1, 9):
        for way in range(2):
            last = 8 if way == 0 else 7
            if step > last:
                continue
            onward = hop(step + 1, way) if step < last else None
            for p in range(2):
                flying[way][p].wait_recv()
                if onward is not None:
                    onward[p].start()
                    started.append(onward[p])
            flying[way] = onward
        if step % 2 == 0:
            b = step // 2 - 1
            xdone[b] = stage_x(b)
            if b >= 1:
                ydone[b - 1] = stage_y(b - 1, xdone[b - 1])
            if b >= 2:
                cdone[b - 2] = stage_c(b - 2, ydone[b - 2])
    ydone[NB - 1] = stage_y(NB - 1, xdone[NB - 1])
    cdone[NB - 2] = stage_c(NB - 2, ydone[NB - 2])
    cdone[NB - 1] = stage_c(NB - 1, ydone[NB - 1])
    for b in range(NB):
        cdone[b].wait_recv()
    for copy in started:
        copy.wait_send()
    for b in range(NB):
        for copy in xdone[b][0] + ydone[b][0] + [cdone[b]]:
            copy.wait_send()


def return_kernel(
    parts_ref, codes_ref, rmat_ref, out_ref,
    cb, ys, yr, q, xb, dense, ring_out, ring_in, total, select,
    c_send, c_recv, y_send, y_recv, x_send, x_recv, z_send, z_recv, a_send, a_recv, local,
):
    e, t, z, x, y, c = place()
    phi = c * NY + y
    half = y // 2
    greet(e, t, z, x)
    started = []
    order = list(range(NB - 1, -1, -1))

    core = {}
    for b in order:
        copy = remote(
            parts_ref.at[
                :, pl.ds(b * ROWS, ROWS),
                pl.ds(pl.multiple_of((1 - c) * (NY * FEAT), NY * FEAT), NY * FEAT),
            ],
            cb.at[b], c_send.at[b], c_recv.at[b], (e, y * NC + 1 - c),
        )
        copy.start()
        core[b] = copy
        started.append(copy)

    def stage_y(b):
        core[b].wait_recv()
        for k in range(NY):
            mine = parts_ref[
                :, pl.ds(b * ROWS, ROWS), pl.ds(pl.multiple_of((c * NY + k) * FEAT, FEAT), FEAT)
            ]
            theirs = cb[b, :, :, k * FEAT : (k + 1) * FEAT]
            ys[b, k] = (mine.astype(F32) + theirs.astype(F32)).astype(BF)
        sent = []
        for i in range(1, NY):
            other = lax.rem(y + i, NY)
            n = b * (NY - 1) + i - 1
            copy = remote(
                ys.at[b, other], yr.at[b, i - 1], y_send.at[n], y_recv.at[n], (e, other * NC + c)
            )
            copy.start()
            sent.append(copy)
            started.append(copy)
        return sent

    def stage_x(b, sent):
        for copy in sent:
            copy.wait_recv()
        odd = lax.rem(y, 2)
        partner = 2 * (1 - odd)
        q[b, half] = (ys[b, y].astype(F32) + yr[b, partner].astype(F32)).astype(BF)
        q[b, 1 - half] = (yr[b, 1].astype(F32) + yr[b, 2 * odd].astype(F32)).astype(BF)
        copies = []
        for i in range(1, NX):
            other = lax.rem(x + i, NX)
            n = b * (NX - 1) + i - 1
            copy = remote(
                q.at[b, :, :, pl.ds(pl.multiple_of(other * CHUNK, 16), CHUNK), :], xb.at[b, x],
                x_send.at[n], x_recv.at[n], (z * NX + other, t),
            )
            copy.start()
            copies.append(copy)
            started.append(copy)
        stay = pltpu.make_async_copy(
            q.at[b, :, :, pl.ds(pl.multiple_of(x * CHUNK, 16), CHUNK), :], xb.at[b, x], local.at[b]
        )
        stay.start()
        return copies, stay

    def spread(b, earlier):
        copies, stay = earlier
        fill_select(codes_ref[b], rmat_ref[...], select)
        for copy in copies:
            copy.wait_recv()
        stay.wait()
        over = (((0,), (0,)), ((), ()))
        outs = xb[b, :, :, 0].reshape(SLOTS, FEAT)
        grads = xb[b, :, :, 1].reshape(SLOTS, FEAT)
        first = lax.dot_general(select[1], outs, over, preferred_element_type=F32)
        first = first + lax.dot_general(select[2], outs, over, preferred_element_type=F32)
        second = lax.dot_general(select[0], grads, over, preferred_element_type=F32)
        for j in range(BATCH):
            dense[b * BATCH + j, 0] = first[j * TOK : (j + 1) * TOK]
            dense[b * BATCH + j, 1] = second[j * TOK : (j + 1) * TOK]

    right = (lax.rem(z + 1, NZ) * NX + x, t)
    left = (lax.rem(z + NZ - 1, NZ) * NX + x, t)
    ring = {}

    def hop(step, way):
        n = way * 8 + step
        slot = SLOT_OF[8 - step] if way == 0 else SLOT_OF[-(7 - step)]
        for arr in range(2):
            value = dense[slot, arr]
            if step > 0:
                ring[way, step - 1, arr].wait_recv()
                value = value + ring_in[n - 1, arr].astype(F32)
            ring_out[n, arr] = value.astype(BF)
            copy = remote(
                ring_out.at[n, arr], ring_in.at[n, arr], z_send.at[2 * n + arr], z_recv.at[2 * n + arr],
                right if way == 0 else left,
            )
            copy.start()
            ring[way, step, arr] = copy
            started.append(copy)

    ysent, xsent = {}, {}
    for b in order:
        ysent[b] = stage_y(b)
    xsent[3] = stage_x(3, ysent[3])
    for n, b in enumerate(order):
        if b > 0:
            xsent[b - 1] = stage_x(b - 1, ysent[b - 1])
        spread(b, xsent[b])
        for step in (2 * n, 2 * n + 1):
            hop(step, 0)
            if step < 7:
                hop(step, 1)
    finals = []
    for arr in range(2):
        ring[0, 7, arr].wait_recv()
        ring[1, 6, arr].wait_recv()
        total[arr] = dense[0, arr] + ring_in[7, arr].astype(F32) + ring_in[8 + 6, arr].astype(F32)
        spot = pl.ds(pl.multiple_of(phi * FEAT, FEAT), FEAT)
        for i in range(1, NT):
            other = lax.rem(t + i, NT)
            n = arr * (NT - 1) + i - 1
            copy = remote(
                total.at[arr, pl.ds(pl.multiple_of(other * OWN, OWN), OWN), :], out_ref.at[arr, :, spot],
                a_send.at[n], a_recv.at[n], (e, other),
            )
            copy.start()
            finals.append(copy)
        stay = pltpu.make_async_copy(
            total.at[arr, pl.ds(pl.multiple_of(t * OWN, OWN), OWN), :], out_ref.at[arr, :, spot],
            local.at[NB + arr],
        )
        stay.start()
        stay.wait()
    for copy in finals:
        copy.wait_recv()
    for copy in started + finals:
        copy.wait_send()


def vmem():
    return pl.BlockSpec(memory_space=pltpu.VMEM)


def dma(*counts):
    return [pltpu.SemaphoreType.DMA((n,)) for n in counts for _ in range(2)]


def constants():
    lane = np.arange(WIDE)
    row = np.arange(CHUNK)
    rmat = np.where(lane[None, :] // TOK == row[:, None] // CAP, row[:, None] % CAP, -5)
    tri = np.arange(TOK)[:, None] < np.arange(TOK)[None, :]
    return jnp.asarray(rmat, F32), jnp.asarray(tri, BF)


def dispatch(own, meta, rmat, tri):
    width = NT * FEAT
    return pl.pallas_call(
        dispatch_kernel,
        out_shape=(
            jax.ShapeDtypeStruct((2, NB * ROWS, width), BF),
            jax.ShapeDtypeStruct((NB, 24, WIDE), F32),
        ),
        in_specs=[vmem()] * 4,
        out_specs=(vmem(), vmem()),
        scratch_shapes=[
            pltpu.VMEM((NZ, 2 * TOK + OWN, FEAT), BF),
            pltpu.VMEM((NB, NX, 2, 2, CHUNK, FEAT), BF),
            pltpu.VMEM((NB, 2, 2, ROWS, FEAT), BF),
            pltpu.VMEM((3, SLOTS, WIDE), BF),
            *dma(2 * (NT - 1), 32, NB * (NX - 1), NB * (NY - 1), NB),
            pltpu.SemaphoreType.DMA((2 + 2 * NB,)),
        ],
        compiler_params=pltpu.CompilerParams(
            collective_id=0, has_side_effects=True, vmem_limit_bytes=48 * 2**20
        ),
        name="dispatch",
    )(own, meta, rmat, tri)


def give_back(parts, codes, rmat):
    width = NT * FEAT
    return pl.pallas_call(
        return_kernel,
        out_shape=jax.ShapeDtypeStruct((2, OWN, width), F32),
        in_specs=[vmem()] * 3,
        out_specs=vmem(),
        scratch_shapes=[
            pltpu.VMEM((NB, 2, ROWS, NY * FEAT), BF),
            pltpu.VMEM((NB, NY, 2, ROWS, FEAT), BF),
            pltpu.VMEM((NB, NY - 1, 2, ROWS, FEAT), BF),
            pltpu.VMEM((NB, 2, 2, ROWS, FEAT), BF),
            pltpu.VMEM((NB, NX, 2, 2, CHUNK, FEAT), BF),
            pltpu.VMEM((NZ, 2, TOK, FEAT), F32),
            pltpu.VMEM((NZ, 2, TOK, FEAT), BF),
            pltpu.VMEM((NZ, 2, TOK, FEAT), BF),
            pltpu.VMEM((2, TOK, FEAT), F32),
            pltpu.VMEM((3, SLOTS, WIDE), BF),
            *dma(NB, NB * (NY - 1), NB * (NX - 1), 32, 2 * (NT - 1)),
            pltpu.SemaphoreType.DMA((NB + 2,)),
        ],
        compiler_params=pltpu.CompilerParams(
            collective_id=1, has_side_effects=True, vmem_limit_bytes=56 * 2**20
        ),
        name="give_back",
    )(parts, codes, rmat)


def shards(tokens, cotangent, gain, expert_ids, gate_probs, gate_up_weight, down_weight):
    z = lax.axis_index("expert") // NX
    t = lax.axis_index("tensor")
    values = tokens.astype(F32)
    inv_rms = lax.rsqrt(jnp.mean(values * values, axis=1, keepdims=True) + 1e-06)
    scaled = values * inv_rms
    normed = (scaled * gain[None, :]).astype(BF)
    own = jnp.stack([normed, cotangent])
    probs_t = gate_probs.T
    high = probs_t.astype(BF)
    low = (probs_t - high.astype(F32)).astype(BF)
    meta = jnp.concatenate(
        [
            jnp.concatenate([expert_ids.T.astype(BF), high], axis=0),
            jnp.concatenate([low, jnp.zeros_like(low)], axis=0),
        ],
        axis=1,
    )
    rmat, tri = constants()
    routed, codes = dispatch(own, meta, rmat, tri)
    rows, slot_grads = routed[0], routed[1]

    gate_up, down_proj = gate_up_weight[0], down_weight[0]
    width = down_proj.shape[0]
    projected = jnp.dot(rows, gate_up, preferred_element_type=F32)
    gate_pre, up_pre = projected[:, :width], projected[:, width:]
    sig = jax.nn.sigmoid(gate_pre)
    hidden = (gate_pre * sig * up_pre).astype(BF)
    block_out = jnp.dot(hidden, down_proj, preferred_element_type=F32).astype(BF)
    hidden_grad = lax.dot_general(slot_grads, down_proj, (((1,), (1,)), ((), ())), preferred_element_type=F32)
    prob_slots = jnp.sum(hidden_grad * hidden.astype(F32), axis=1)
    joined = jnp.concatenate(
        [
            (hidden_grad * up_pre * sig * (1.0 + gate_pre * (1.0 - sig))).astype(BF),
            (hidden_grad * gate_pre * sig).astype(BF),
        ],
        axis=1,
    )
    over_rows = (((0,), (0,)), ((), ()))
    input_grad = lax.dot_general(joined, gate_up, (((1,), (1,)), ((), ())), preferred_element_type=F32).astype(BF)
    summed = give_back(jnp.stack([block_out, input_grad]), codes, rmat)
    down_grad = lax.dot_general(hidden, slot_grads, over_rows, preferred_element_type=F32).astype(BF)
    gate_up_sum = lax.dot_general(rows, joined, over_rows, preferred_element_type=F32)
    gate_up_grad = gate_up_sum.astype(BF)

    gain_part = jnp.sum(gate_up.astype(F32) * gate_up_sum, axis=1)
    gain_grad = lax.psum(gain_part, ("expert", "tensor")) / gain

    by_slot = prob_slots.reshape(NB, NX, BATCH, CAP).transpose(0, 2, 1, 3).reshape(NZ, NX * CAP)
    slots = [SLOT_OF[(d + 7) % NZ - 7] for d in range(NZ)]
    by_distance = jnp.concatenate([by_slot[s : s + 1] for s in slots * 2], axis=0)
    by_group = lax.dynamic_slice_in_dim(by_distance, lax.rem(NZ - z, NZ), NZ, axis=0).reshape(NZ * NX, CAP)
    home = lax.all_to_all(by_group, "expert", split_axis=0, concat_axis=0, tiled=True)
    kind = t // NY
    targets = jnp.arange(NZ * NX, dtype=jnp.int32) * 2 + kind
    matches = expert_ids[:, :, None] == targets[None, None, :]
    chosen = jnp.any(matches, axis=1)
    earlier = jnp.arange(TOK)[None, :] < jnp.arange(TOK)[:, None]
    rank = jnp.dot(earlier.astype(BF), chosen.astype(BF), preferred_element_type=F32).astype(jnp.int32)
    picked = rank[:, :, None] == jnp.arange(CAP, dtype=jnp.int32)[None, None, :]
    value = jnp.sum(jnp.where(picked, home[None, :, :], 0.0), axis=2)
    prob_part = jnp.sum(jnp.where(matches, value[:, None, :], 0.0), axis=2)
    prob_sum = lax.psum_scatter(prob_part, "tensor", scatter_dimension=0, tiled=True)
    prob_grad = prob_sum / lax.dynamic_slice_in_dim(gate_probs, t * OWN, OWN, axis=0)

    mixed = (values + summed[0]).astype(BF)
    gain_side = summed[1] * gain[None, :]
    token_grad = (
        cotangent.astype(F32)
        + inv_rms * (gain_side - scaled * jnp.mean(gain_side * scaled, axis=1, keepdims=True))
    ).astype(BF)
    return (mixed, token_grad, prob_grad, gain_grad, gate_up_grad[None], down_grad[None])


def solution(mesh):
    both = P(("expert", "tensor"), None)
    cube = P(("expert", "tensor"), None, None)
    in_specs = (both, both, P(), P("expert", None), P("expert", None), cube, cube)
    out_specs = (both, both, both, P(), cube, cube)
    return jax.shard_map(shards, mesh=mesh, in_specs=in_specs, out_specs=out_specs, check_vma=False)
```

time: 1010 us -> 309 us (0.31)
  waiting for transfers between devices: 692 us -> 0.02 us
  Pallas kernels: 0 us -> 148 us
  local copies, waits for them, and re-layouts: 64.5 us -> 7.76 us
  starting transfers between devices: 49.8 us -> 9.55 us
  blocking collectives: 139 us -> 101 us
  matrix products: 30.7 us -> 15.2 us
    all_to_all x4 -> x1, waiting for transfers between devices: 669 us -> 0.01 us  [shards(): lax.all_to_all(by_group, 'expert', split_axis=0, concat_axis=0, tiled=True)]
    pallas_call x0 -> x2, Pallas kernels: none -> 148 us  [the longest x1 77 us: dispatch(): pl.pallas_call(dispatch_kernel, out_shape=(jax.ShapeDtypeStruct((2, NB *...]
    all_to_all x4 -> x1, starting transfers between devices: 49.7 us -> 9.32 us  [shards(): lax.all_to_all(by_group, 'expert', split_axis=0, concat_axis=0, tiled=True)]
    reshape x7 -> x2, local copies, waits for them, and re-layouts: 36.9 us -> 0.19 us  [shards(): prob_slots.reshape(NB, NX, BATCH, CAP).transpose(0, 2, 1, 3)]
    all_gather x2 -> x0, blocking collectives: 33.2 us -> none  [the longest x1 19.8 us: shards(): lax.all_gather(carried, 'tensor', axis=0, tiled=True)]
    gather x5 -> x0, local copies, waits for them, and re-layouts: 25 us -> none  [the longest x2 10.4 us: shards(): jnp.take(group_grads, source, axis=0).astype(jnp.float32)]
    reduce_scatter x2 -> x0, waiting for transfers between devices: 23.3 us -> none  [the longest x1 23.3 us: shards(): lax.psum_scatter(input_part, 'tensor', scatter_dimension=0, tiled=True)]
    dot_general x9 -> x7, matrix products: 29.6 us -> 15.2 us  [the longest x1 3.92 us: shards(): projected = jnp.dot(rows, gate_up, preferred_element_type=F32)]
  transfers between devices with their start and end apart: 7 -> 2, of which waited for: 5 -> 0; matrix products, arithmetic and copies ran while one was open for 7% -> 6% of each run, Pallas kernels for 0% -> 23%
where the time goes in v1:
time: 309 us
  Pallas kernels  148 us (48%)
  blocking collectives  101 us (33%)
  matrix products  15.2 us (5%)
  between operations  14.3 us (5%)
  other arithmetic  11.9 us (4%)
  starting transfers between devices  9.55 us (3%)
  local copies, waits for them, and re-layouts  7.76 us (3%)
    psum x1, blocking collectives, shards(): gain_grad = lax.psum(gain_part, ('expert', 'tensor')) / gain  101 us
    pallas_call x1, Pallas kernels, dispatch(): pl.pallas_call(dispatch_kernel, out_shape=(jax.ShapeDtypeStruct((2, NB *...  77 us
    pallas_call x1, Pallas kernels, give_back(): pl.pallas_call(return_kernel, out_shape=jax.ShapeDtypeStruct((2, OWN, wid...  71.3 us
    all_to_all x1, starting transfers between devices, shards(): lax.all_to_all(by_group, 'expert', split_axis=0, concat_axis=0, tiled=True)  9.32 us
    unnamed x28, local copies, waits for them, and re-layouts  6.68 us
  transfers between devices with their start and end apart: 2, of which 0 were waited for; matrix products, arithmetic and copies ran while one was open for 6% of the time, Pallas kernels for 23%

profile of v1, /device:TPU:1, one launch (start us, length us, event | category | flops | bytes accessed | tf_op | source)
XLA Modules:
  0.0 308.5 jit_solution(9537821892701689233)
XLA Ops:
  7.2 1.0 fusion.34
  8.2 0.7 convert_bitcast_fusion.1
  8.9 0.7 fusion.39
  9.6 0.9 fusion.36
  10.6 0.9 pad_maximum_fusion.4.own_ref
  11.4 0.9 copy-done.1
  12.3 0.8 copy-done.3
  13.1 77.0 %dispatch.1 = (bf16[2,768,2048]{2,1,0:T(8,128)(2,1)}, f32[4,24,512]{2,1,0:T(8,128)S(1)}) custom-call(bf16[2,16,2048]{2,1,0:T(8,128)(2,1)S(1)} %pad_maximum_fusion.4.own_ref, bf16[16,256]{1,0:T(8,128)(2,1)S(1)} %fusion.38.meta_ref, f32[48,512]{1,0:T(8,128)S(1)} %copy-done.1, bf16[128,128]{1,0:T(8,128)(2,1)S(1)} %copy-done.3), custom_call_target="tpu_custom_call" | custom-call | tf_op jit(solution)/shard_map/dispatch/pallas_call | solution.py:400
  90.2 3.9 %fusion.6 = f32[768,384]{0,1:T(8,128)S(1)} fusion(bf16[2,768,2048]{2,1,0:T(8,128)(2,1)} %get-tuple-element.8, bf16[1,2048,384]{2,1,0:T(8,128)(2,1)} %param.14), kind=kOutput, calls=%fused_computation.9 | convolution fusion | flops 1207959552 | bytes 5898240 | tf_op jit(solution)/shard_map/dot_general | solution.py:475
  94.1 0.3 copy-done.11
  94.4 1.4 multiply_reduce_fusion.1
  95.8 0.1 reshape.45
  96.2 0.7 all_to_all.6
  96.8 9.3 %all-to-all-start = ((f32[64,1,12]{2,1,0:T(1,128)}), f32[64,1,12]{2,1,0:T(1,128)S(1)}, u32[]{:S(2)}, u32[]{:S(2)}) async-start(f32[64,1,12]{2,1,0:T(1,128)} %bitcast.13), calls=%async_computation | async-start | bytes 65536 | tf_op jit(solution)/shard_map/all_to_all | solution.py:503
  106.2 0.2 reduce-scatter.4.cloned.1.call-start
  106.4 1.6 copy.34
  108.2 1.9 fusion.8
  110.0 3.4 %convert_bitcast_fusion = (bf16[1,2048,384]{1,2,0:T(8,128)(2,1)S(1)}, f32[2048]{0:T(1024)S(1)}) fusion(bf16[1,2048,384]{1,2,0:T(8,128)(2,1)S(1)} %copy-done.5, bf16[2,768,2048]{2,1,0:T(8,128)(2,1)} %get-tuple-element.8, bf16[768,192]{0,1:T(8,128)(2,1)S(1)} %get-tuple-element.46, bf16[768,192]{0,1:T(8,128)(2,1)S(1)} %get-tuple-element.47), kind=kOutput, calls=%fused_computation.22 | convolution fusion | flops 1212282880 | bytes 6889472 | tf_op jit(solution)/shard_map/dot_general | solution.py:493
  113.4 1.0 fusion.9
  114.4 3.2 %pad_maximum_fusion.parts_ref = bf16[2,768,2048]{2,1,0:T(8,128)(2,1)} fusion(bf16[1,768,2048]{2,1,0:T(8,128)(2,1)S(1)} %fusion.8, bf16[1,768,2048]{2,1,0:T(8,128)(2,1)S(1)} %fusion.9), kind=kLoop, calls=%fused_computation | loop fusion | flops 3145728 | bytes 12582912 | tf_op jit(solution)/shard_map/stack | solution.py:491
  117.6 71.3 %give_back.1 = f32[2,16,2048]{2,1,0:T(8,128)} custom-call(bf16[2,768,2048]{2,1,0:T(8,128)(2,1)} %pad_maximum_fusion.parts_ref, f32[4,24,512]{2,1,0:T(8,128)} %copy-done.2, f32[48,512]{1,0:T(8,128)} %constant.61.clone.rmat_ref), custom_call_target="tpu_custom_call" | custom-call | tf_op jit(solution)/shard_map/give_back/pallas_call | solution.py:425
  188.9 1.1 fusion.29
  190.1 1.7 fusion.33
  191.8 0.1 convolution_convert_fusion.2
  192.0 0.2 select_reduce_fusion
  192.3 0.7 copy.39
  193.1 3.6 %fusion.17 = bf16[1,192,2048]{2,1,0:T(8,128)(2,1)} fusion(bf16[768,192]{0,1:T(8,128)(2,1)S(1)} %get-tuple-element.41, bf16[2,768,2048]{2,1,0:T(8,128)(2,1)} %get-tuple-element.8), kind=kOutput, calls=%fused_computation.19 | convolution fusion | flops 604372992 | bytes 4227072 | tf_op jit(solution)/shard_map/dot_general | solution.py:492
  196.6 1.6 copy.38
  198.2 101.4 %psum.7 = f32[2048]{0:T(1024)S(1)} all-reduce(f32[2048]{0:T(1024)S(1)} %get-tuple-element.45), channel_id=1, replica_groups=mesh['expert'=64,'tensor'=8] {'expert','tensor'}, use_global_device_ids=true, to_apply=%region_8.9 | all-reduce | flops 2048 | bytes 16384 | tf_op jit(solution)/shard_map/psum | solution.py:497
  299.6 0.6 div.40
  300.2 0.8 copy.40
  301.0 0.7 dynamic-slice_divide_fusion
  (37 shorter events, 0.6 us)
Async XLA Ops:
  7.2 86.9 %copy-start = (bf16[1,192,2048]{2,1,0:T(8,128)(2,1)S(1)}, bf16[1,192,2048]{2,1,0:T(8,128)(2,1)}, u32[]{:S(2)}) copy-start(bf16[1,192,2048]{2,1,0:T(8,128)(2,1)} %param.15) | copy-start | bytes 2359300
  11.4 0.9 copy-start.1
  12.3 0.8 copy-start.3
  90.1 4.0 %copy-start.2 = (f32[4,24,512]{2,1,0:T(8,128)}, f32[4,24,512]{2,1,0:T(8,128)S(1)}, u32[]{:S(2)}) copy-start(f32[4,24,512]{2,1,0:T(8,128)S(1)} %get-tuple-element.9.codes_ref) | copy-start | bytes 589828
  90.1 4.3 %copy-start.11 = (bf16[2,768,2048]{2,1,0:T(8,128)(2,1)S(1)}, bf16[2,768,2048]{2,1,0:T(8,128)(2,1)}, u32[]{:S(2)}) copy-start(bf16[2,768,2048]{2,1,0:T(8,128)(2,1)} %get-tuple-element.8) | copy-start | bytes 18874372
  94.4 12.0 %copy-start.4 = (bf16[1,2048,384]{2,1,0:T(8,128)(2,1)S(1)}, bf16[1,2048,384]{2,1,0:T(8,128)(2,1)}, u32[]{:S(2)}) copy-start(bf16[1,2048,384]{2,1,0:T(8,128)(2,1)} %param.14) | copy-start | bytes 4718596
  95.8 12.2 %copy-start.9 = (s32[128,8]{0,1:T(8,128)S(1)}, s32[128,8]{0,1:T(8,128)}, u32[]{:S(2)}) copy-start(s32[128,8]{0,1:T(8,128)} %param.12) | copy-start | bytes 12292
  96.8 95.1 %all-to-all-start = ((f32[64,1,12]{2,1,0:T(1,128)}), f32[64,1,12]{2,1,0:T(1,128)S(1)}, u32[]{:S(2)}, u32[]{:S(2)}) async-start(f32[64,1,12]{2,1,0:T(1,128)} %bitcast.13), calls=%async_computation | async-start | bytes 65536 | tf_op jit(solution)/shard_map/all_to_all | solution.py:503
  106.2 194.0 %reduce-scatter.4.cloned.1.call-start = ((), (), s32[]{:S(2)}) async-start(), calls=%async_computation.2 | async-start | bytes 73728
  108.2 1.9 copy-start.5
  117.6 71.3 %copy-start.6 = (bf16[16,2048]{1,0:T(8,128)(2,1)S(1)}, bf16[16,2048]{1,0:T(8,128)(2,1)}, u32[]{:S(2)}) copy-start(bf16[16,2048]{1,0:T(8,128)(2,1)} %param.9) | copy-start | bytes 196612
  117.6 71.3 %copy-start.8 = (f32[2048]{0:T(1024)S(1)}, f32[2048]{0:T(1024)}, u32[]{:S(2)}) copy-start(f32[2048]{0:T(1024)} %param.11) | copy-start | bytes 24580
  117.6 72.4 %copy-start.7 = (bf16[16,2048]{1,0:T(8,128)(2,1)S(1)}, bf16[16,2048]{1,0:T(8,128)(2,1)}, u32[]{:S(2)}) copy-start(bf16[16,2048]{1,0:T(8,128)(2,1)} %param.10) | copy-start | bytes 196612
  193.0 107.9 %copy-start.10 = (f32[128,8]{0,1:T(8,128)S(1)}, f32[128,8]{0,1:T(8,128)}, u32[]{:S(2)}) copy-start(f32[128,8]{0,1:T(8,128)} %param.13) | copy-start | bytes 12292
Sparse Core Ops, SparseCore 0:
  193.2 30.8 reduce-scatter.3

commit v2 on v1

v2 whole, which is shorter than its diff:
```python
import jax
import jax.numpy as jnp
import numpy as np
from jax import lax
from jax.experimental import pallas as pl
from jax.experimental.pallas import tpu as pltpu
from jax.sharding import PartitionSpec as P

TOP = 8
NZ, NX, NY, NC = 16, 4, 4, 2
NT = NY * NC
TOK = 128
OWN = 16
CAP = 12
FEAT = 256
BATCH = 4
NB = NZ // BATCH
CHUNK = BATCH * CAP
ROWS = NX * CHUNK
SLOTS = NX * 2 * CHUNK
WIDE = BATCH * TOK
ORDER = [0, 1, -1, 2, -2, 3, -3, 4, -4, 5, -5, 6, -6, 7, -7, 8]
SLOT_OF = {d: s for s, d in enumerate(ORDER)}
SLOT_OF[-8] = SLOT_OF[8]
BF, F32 = jnp.bfloat16, jnp.float32
ACROSS = (((1,), (1,)), ((), ()))
OVER = (((0,), (0,)), ((), ()))


def place():
    e, t = lax.axis_index("expert"), lax.axis_index("tensor")
    return e, t, e // NX, lax.rem(e, NX), t // NC, lax.rem(t, NC)


def remote(src, dst, send, recv, device):
    return pltpu.make_async_remote_copy(
        src_ref=src, dst_ref=dst, send_sem=send, recv_sem=recv,
        device_id=device, device_id_type=pl.DeviceIdType.MESH,
    )


def greet(e, t, z, x):
    barrier = pltpu.get_barrier_semaphore()
    peers = [(e, lax.rem(t + i, NT)) for i in range(1, NT)]
    peers += [(z * NX + lax.rem(x + i, NX), t) for i in range(1, NX)]
    peers += [(lax.rem(z + i, NZ) * NX + x, t) for i in (1, NZ - 1)]
    for peer in peers:
        pl.semaphore_signal(barrier, inc=1, device_id=peer, device_id_type=pl.DeviceIdType.MESH)
    pl.semaphore_wait(barrier, len(peers))


def experts_kernel(
    normed_ref, cot_ref, meta_ref, rmat_ref, tri_ref, up_ref, down_ref,
    out_ref, prob_ref, gain_ref, up_grad_ref, down_grad_ref,
    zbuf, xs, yb, select, routed, parts, hid, joined,
    cb, ys, yr, q, xb, dense, ring_out, ring_in, total,
    pdense, pring_out, pring_in, ptotal, pgot, gsend, gone, gx, gz,
    a_send, a_recv, z_send, z_recv, x_send, x_recv, y_send, y_recv, c_send, c_recv,
    c2_send, c2_recv, y2_send, y2_recv, x2_send, x2_recv, z2_send, z2_recv, a2_send, a2_recv,
    p_send, p_recv, pa_send, pa_recv, g1_send, g1_recv, g2_send, g2_recv, g3_send, g3_recv,
    g4_send, g4_recv, local,
):
    e, t, z, x, y, c = place()
    phi = c * NY + y
    half = y // 2
    width = hid.shape[1]
    greet(e, t, z, x)
    started = []

    def feat(index):
        return pl.ds(pl.multiple_of(index * FEAT, FEAT), FEAT)

    def core_half(index):
        return pl.ds(pl.multiple_of(index * (NY * FEAT), NY * FEAT), NY * FEAT)

    def block16(index, size):
        return pl.ds(pl.multiple_of(index * size, 16), size)

    def go(src, dst, send, recv, n, device):
        copy = remote(src, dst, send.at[n], recv.at[n], device)
        copy.start()
        started.append(copy)
        return copy

    def others():
        return [(i, lax.rem(t + i, NT)) for i in range(1, NT)]

    def phi_of(other):
        return lax.rem(other, NC) * NY + other // NC

    right = (lax.rem(z + 1, NZ) * NX + x, t)
    left = (lax.rem(z + NZ - 1, NZ) * NX + x, t)

    stays = []
    arrivals = []
    for arr, ref in enumerate((normed_ref, cot_ref)):
        row_at = block16(arr * (TOK // OWN) + t, OWN)
        for i, other in others():
            n = arr * (NT - 1) + i - 1
            arrivals.append(
                go(ref.at[:, feat(phi_of(other))], zbuf.at[0, row_at, :], a_send, a_recv, n, (e, other))
            )
        stay = pltpu.make_async_copy(ref.at[:, feat(phi)], zbuf.at[0, row_at, :], local.at[arr])
        stay.start()
        stays.append(stay)
    zbuf[0, 2 * TOK :, :] = meta_ref[...]
    for copy in arrivals:
        copy.wait_recv()
    for stay in stays:
        stay.wait()

    pieces = (pl.ds(0, TOK), pl.ds(TOK, TOK + OWN))

    def hop(step, way, p):
        sign = -1 if way == 0 else 1
        src, dst = SLOT_OF[sign * (step - 1)], SLOT_OF[sign * step]
        return go(
            zbuf.at[src, pieces[p], :], zbuf.at[dst, pieces[p], :], z_send, z_recv,
            (way * 8 + step - 1) * 2 + p, right if way == 0 else left,
        )

    def named_experts():
        base = lax.convert_element_type(z * (2 * NX), F32)
        return base + lax.broadcasted_iota(jnp.int32, (8, TOK), 0).astype(F32)

    def stage_x(b):
        named = named_experts()
        chosen, high, low = [], [], []
        for j in range(BATCH):
            meta = zbuf[b * BATCH + j, 2 * TOK :, :].astype(F32)
            got, hi, lo = jnp.zeros((8, TOK), F32), jnp.zeros((8, TOK), F32), jnp.zeros((8, TOK), F32)
            for k in range(TOP):
                same = meta[k : k + 1, :TOK] == named
                got = got + jnp.where(same, 1.0, 0.0)
                hi = hi + jnp.where(same, meta[8 + k : 9 + k, :TOK], 0.0)
                lo = lo + jnp.where(same, meta[k : k + 1, TOK:], 0.0)
            chosen.append(got)
            high.append(hi)
            low.append(lo)
        taken = jnp.concatenate(chosen, axis=0)
        rank = jnp.dot(taken.astype(BF), tri_ref[...], preferred_element_type=F32)
        code = jnp.where(taken > 0.5, rank, -1.0)
        codes = jnp.concatenate(
            [
                jnp.concatenate([code[8 * j : 8 * j + 8] for j in range(BATCH)], axis=1),
                jnp.concatenate(high, axis=1),
                jnp.concatenate(low, axis=1),
            ],
            axis=0,
        )
        for f in range(2 * NX):
            hit = codes[f : f + 1, :] == rmat_ref[...]
            rows = pl.ds(f * CHUNK, CHUNK)
            select[b, 0, rows, :] = jnp.where(hit, 1.0, 0.0).astype(BF)
            select[b, 1, rows, :] = jnp.where(hit, codes[8 + f : 9 + f, :], 0.0).astype(BF)
            select[b, 2, rows, :] = jnp.where(hit, codes[16 + f : 17 + f, :], 0.0).astype(BF)
        these = pl.ds(b * BATCH, BATCH)
        normed = zbuf[these, 0:TOK, :].reshape(WIDE, FEAT)
        cot = zbuf[these, TOK : 2 * TOK, :].reshape(WIDE, FEAT)
        picked = jnp.dot(select[b, 0], normed, preferred_element_type=F32).astype(BF)
        grads = (
            jnp.dot(select[b, 1], cot, preferred_element_type=F32)
            + jnp.dot(select[b, 2], cot, preferred_element_type=F32)
        ).astype(BF)
        xs[b, :, :, 0] = picked.reshape(NX, 2, CHUNK, FEAT)
        xs[b, :, :, 1] = grads.reshape(NX, 2, CHUNK, FEAT)
        at = block16(x, CHUNK)
        copies = []
        for i in range(1, NX):
            other = lax.rem(x + i, NX)
            copies.append(
                go(
                    xs.at[b, other], yb.at[b, :, :, at, :], x_send, x_recv,
                    b * (NX - 1) + i - 1, (z * NX + other, t),
                )
            )
        stay = pltpu.make_async_copy(xs.at[b, x], yb.at[b, :, :, at, :], local.at[2 + b])
        stay.start()
        return copies, stay

    def stage_y(b, earlier):
        copies, stay = earlier
        for copy in copies:
            copy.wait_recv()
        stay.wait()
        where = pl.ds(b * ROWS, ROWS)
        sent = []
        for i in range(1, NY):
            other = lax.rem(y + i, NY)
            sent.append(
                go(
                    yb.at[b, other // 2], routed.at[:, where, feat(phi)], y_send, y_recv,
                    b * (NY - 1) + i - 1, (e, other * NC + c),
                )
            )
        keep = pltpu.make_async_copy(yb.at[b, half], routed.at[:, where, feat(phi)], local.at[2 + NB + b])
        keep.start()
        return sent, keep

    def stage_c(b, earlier):
        sent, keep = earlier
        for copy in sent:
            copy.wait_recv()
        keep.wait()
        block = routed.at[:, pl.ds(b * ROWS, ROWS), core_half(c)]
        return go(block, block, c_send, c_recv, b, (e, y * NC + 1 - c))

    def compute(b, earlier):
        earlier.wait_recv()
        where = pl.ds(b * ROWS, ROWS)
        projected = jnp.dot(routed[0, where, :], up_ref[...], preferred_element_type=F32)
        gate_pre, up_pre = projected[:, :width], projected[:, width:]
        sig = jax.nn.sigmoid(gate_pre)
        hidden = (gate_pre * sig * up_pre).astype(BF)
        hid[where, :] = hidden
        hidden_grad = lax.dot_general(routed[1, where, :], down_ref[...], ACROSS, preferred_element_type=F32)
        both = jnp.concatenate(
            [
                hidden_grad * up_pre * sig * (1.0 + gate_pre * (1.0 - sig)),
                hidden_grad * gate_pre * sig,
            ],
            axis=1,
        ).astype(BF)
        joined[where, :] = both
        for n in range(4):
            cols = pl.ds(n * 2 * FEAT, 2 * FEAT)
            parts[0, where, cols] = jnp.dot(hidden, down_ref[:, cols], preferred_element_type=F32).astype(BF)
            parts[1, where, cols] = lax.dot_general(
                both, up_ref[cols, :], ACROSS, preferred_element_type=F32
            ).astype(BF)
        return go(parts.at[:, where, core_half(1 - c)], cb.at[b], c2_send, c2_recv, b, (e, y * NC + 1 - c))

    def weight_grads():
        for n in range(4):
            cols = pl.ds(n * 2 * FEAT, 2 * FEAT)
            down_grad_ref[:, cols] = lax.dot_general(
                hid[...], routed[1, :, cols], OVER, preferred_element_type=F32
            ).astype(BF)
            grad = lax.dot_general(routed[0, :, cols], joined[...], OVER, preferred_element_type=F32)
            up_grad_ref[cols, :] = grad.astype(BF)
            summed = lax.dot_general(
                jnp.ones((8, 2 * width), F32), grad * up_ref[cols, :].astype(F32), ACROSS,
                precision=lax.Precision.HIGHEST, preferred_element_type=F32,
            )
            gsend[2 * n] = summed[:, :FEAT]
            gsend[2 * n + 1] = summed[:, FEAT:]

    def back_y(b, earlier):
        earlier.wait_recv()
        for k in range(NY):
            mine = parts[:, pl.ds(b * ROWS, ROWS), feat(c * NY + k)]
            theirs = cb[b, :, :, k * FEAT : (k + 1) * FEAT]
            ys[b, k] = (mine.astype(F32) + theirs.astype(F32)).astype(BF)
        sent = []
        for i in range(1, NY):
            other = lax.rem(y + i, NY)
            sent.append(
                go(
                    ys.at[b, other], yr.at[b, i - 1], y2_send, y2_recv,
                    b * (NY - 1) + i - 1, (e, other * NC + c),
                )
            )
        return sent

    def back_x(b, sent):
        for copy in sent:
            copy.wait_recv()
        odd = lax.rem(y, 2)
        partner = 2 * (1 - odd)
        q[b, half] = (ys[b, y].astype(F32) + yr[b, partner].astype(F32)).astype(BF)
        q[b, 1 - half] = (yr[b, 1].astype(F32) + yr[b, 2 * odd].astype(F32)).astype(BF)
        copies = []
        for i in range(1, NX):
            other = lax.rem(x + i, NX)
            copies.append(
                go(
                    q.at[b, :, :, block16(other, CHUNK), :], xb.at[b, x], x2_send, x2_recv,
                    b * (NX - 1) + i - 1, (z * NX + other, t),
                )
            )
        stay = pltpu.make_async_copy(
            q.at[b, :, :, block16(x, CHUNK), :], xb.at[b, x], local.at[2 + 2 * NB + b]
        )
        stay.start()
        return copies, stay

    def spread(b, earlier):
        copies, stay = earlier
        these = pl.ds(b * BATCH, BATCH)
        cot = zbuf[these, TOK : 2 * TOK, :].reshape(WIDE, FEAT)
        cot_slots = jnp.dot(select[b, 0], cot, preferred_element_type=F32)
        for copy in copies:
            copy.wait_recv()
        stay.wait()
        outs = xb[b, :, :, 0].reshape(SLOTS, FEAT)
        grads = xb[b, :, :, 1].reshape(SLOTS, FEAT)
        first = lax.dot_general(select[b, 1], outs, OVER, preferred_element_type=F32)
        first = first + lax.dot_general(select[b, 2], outs, OVER, preferred_element_type=F32)
        second = lax.dot_general(select[b, 0], grads, OVER, preferred_element_type=F32)
        for j in range(BATCH):
            dense[b * BATCH + j, 0] = first[j * TOK : (j + 1) * TOK]
            dense[b * BATCH + j, 1] = second[j * TOK : (j + 1) * TOK]
        value = jnp.sum(cot_slots * outs.astype(F32), axis=1, keepdims=True)
        by_expert = jnp.concatenate(
            [
                jnp.sum(
                    select[b, 0, f * CHUNK : (f + 1) * CHUNK, :].astype(F32)
                    * value[f * CHUNK : (f + 1) * CHUNK],
                    axis=0, keepdims=True,
                )
                for f in range(2 * NX)
            ],
            axis=0,
        )
        named = named_experts()
        for j in range(BATCH):
            ids = zbuf[b * BATCH + j, 2 * TOK :, :TOK].astype(F32)
            mine = by_expert[:, j * TOK : (j + 1) * TOK]
            pdense[b * BATCH + j] = jnp.concatenate(
                [
                    jnp.sum(jnp.where(ids[k : k + 1] == named, mine, 0.0), axis=0, keepdims=True)
                    for k in range(TOP)
                ],
                axis=0,
            )

    ring = {}

    def back_hop(step, way):
        n = way * 8 + step
        slot = SLOT_OF[8 - step] if way == 0 else SLOT_OF[-(7 - step)]
        device = right if way == 0 else left
        for arr in range(2):
            value = dense[slot, arr]
            if step > 0:
                ring[way, step - 1, arr].wait_recv()
                value = value + ring_in[n - 1, arr].astype(F32)
            ring_out[n, arr] = value.astype(BF)
            ring[way, step, arr] = go(
                ring_out.at[n, arr], ring_in.at[n, arr], z2_send, z2_recv, 2 * n + arr, device
            )
        value = pdense[slot]
        if step > 0:
            ring[way, step - 1, 2].wait_recv()
            ring[way, step - 1, 3].wait_recv()
            value = value + pring_in[n - 1]
        pring_out[n] = value
        ring[way, step, 2] = go(pring_out.at[n], pring_in.at[n], p_send, p_recv, n, device)
        origin = lax.rem(z - step + NZ, NZ) if way == 0 else lax.rem(z + step, NZ)
        ring[way, step, 3] = go(gz.at[origin], gz.at[origin], g3_send, g3_recv, n, device)

    flying = {}
    for p in range(2):
        for way in range(2):
            flying[way, p] = hop(1, way, p)
    xdone, ydone, cdone, back = {}, {}, {}, {}
    for step in range(1, 9):
        for p in range(2):
            for way in range(2):
                last = 8 if way == 0 else 7
                if step > last:
                    continue
                flying[way, p].wait_recv()
                if step < last:
                    flying[way, p] = hop(step + 1, way, p)
        if step % 2 == 0:
            b = step // 2 - 1
            xdone[b] = stage_x(b)
            if b >= 1:
                ydone[b - 1] = stage_y(b - 1, xdone[b - 1])
            if b >= 2:
                cdone[b - 2] = stage_c(b - 2, ydone[b - 2])
    ydone[3] = stage_y(3, xdone[3])
    back[0] = compute(0, cdone[0])
    cdone[2] = stage_c(2, ydone[2])
    back[1] = compute(1, cdone[1])
    back[2] = compute(2, cdone[2])
    cdone[3] = stage_c(3, ydone[3])
    back[3] = compute(3, cdone[3])

    ysent = {}
    for b in (3, 2, 1, 0):
        ysent[b] = back_y(b, back[b])
    weight_grads()
    gains = []
    for i, other in others():
        their = phi_of(other)
        gains.append(go(gsend.at[their], gone.at[i], g1_send, g1_recv, i - 1, (e, other)))
    gone[0] = gsend[phi]
    xsent = back_x(3, ysent[3])
    for copy in gains:
        copy.wait_recv()
    gain_sum = gone[0]
    for i in range(1, NT):
        gain_sum = gain_sum + gone[i]
    gx[x] = gain_sum
    gains = []
    for i in range(1, NX):
        other = lax.rem(x + i, NX)
        gains.append(go(gx.at[x], gx.at[x], g2_send, g2_recv, i - 1, (z * NX + other, t)))
    for copy in gains:
        copy.wait_recv()
    gz[z] = gx[0] + gx[1] + gx[2] + gx[3]
    for n, b in enumerate((3, 2, 1, 0)):
        if n > 0:
            xsent = back_x(b, ysent[b])
        spread(b, xsent)
        for step in (2 * n, 2 * n + 1):
            back_hop(step, 0)
            if step < 7:
                back_hop(step, 1)

    finals = []
    for arr in range(2):
        ring[0, 7, arr].wait_recv()
        ring[1, 6, arr].wait_recv()
        total[arr] = dense[0, arr] + ring_in[7, arr].astype(F32) + ring_in[8 + 6, arr].astype(F32)
        for i, other in others():
            n = arr * (NT - 1) + i - 1
            finals.append(
                go(
                    total.at[arr, block16(other, OWN), :], out_ref.at[arr, :, feat(phi)],
                    a2_send, a2_recv, n, (e, other),
                )
            )
        stay = pltpu.make_async_copy(
            total.at[arr, block16(t, OWN), :], out_ref.at[arr, :, feat(phi)], local.at[arr]
        )
        stay.start()
        stays.append(stay)
    for way in range(2):
        for kind in (2, 3):
            ring[way, 7 - way, kind].wait_recv()
    ptotal[...] = pdense[0] + pring_in[7] + pring_in[8 + 6]
    gain_sum = gz[0]
    for n in range(1, NZ):
        gain_sum = gain_sum + gz[n]
    gain_ref[phi] = gain_sum
    for i, other in others():
        finals.append(go(ptotal, pgot.at[i - 1], pa_send, pa_recv, i - 1, (e, other)))
        finals.append(go(gain_ref.at[phi], gain_ref.at[phi], g4_send, g4_recv, i - 1, (e, other)))
    for copy in finals:
        copy.wait_recv()
    for stay in stays[2:]:
        stay.wait()
    prob_sum = ptotal[...]
    for i in range(NT - 1):
        prob_sum = prob_sum + pgot[i]
    prob_ref[...] = prob_sum
    for copy in started:
        copy.wait_send()


def vmem():
    return pl.BlockSpec(memory_space=pltpu.VMEM)


def dma(*counts):
    return [pltpu.SemaphoreType.DMA((n,)) for n in counts for _ in range(2)]


def constants():
    lane = np.arange(WIDE)
    row = np.arange(CHUNK)
    rmat = np.where(lane[None, :] // TOK == row[:, None] // CAP, row[:, None] % CAP, -5)
    tri = np.arange(TOK)[:, None] < np.arange(TOK)[None, :]
    return jnp.asarray(rmat, F32), jnp.asarray(tri, BF)


def experts(normed, cotangent, meta, gate_up, down_proj):
    features, hidden = NT * FEAT, down_proj.shape[0]
    rows = NB * ROWS
    shape = jax.ShapeDtypeStruct
    rmat, tri = constants()
    return pl.pallas_call(
        experts_kernel,
        out_shape=(
            shape((2, OWN, features), F32),
            shape((TOP, TOK), F32),
            shape((NT, 8, FEAT), F32),
            shape((features, 2 * hidden), BF),
            shape((hidden, features), BF),
        ),
        in_specs=[vmem()] * 7,
        out_specs=tuple([vmem()] * 5),
        scratch_shapes=[
            pltpu.VMEM((NZ, 2 * TOK + OWN, FEAT), BF),
            pltpu.VMEM((NB, NX, 2, 2, CHUNK, FEAT), BF),
            pltpu.VMEM((NB, 2, 2, ROWS, FEAT), BF),
            pltpu.VMEM((NB, 3, SLOTS, WIDE), BF),
            pltpu.VMEM((2, rows, features), BF),
            pltpu.VMEM((2, rows, features), BF),
            pltpu.VMEM((rows, hidden), BF),
            pltpu.VMEM((rows, 2 * hidden), BF),
            pltpu.VMEM((NB, 2, ROWS, NY * FEAT), BF),
            pltpu.VMEM((NB, NY, 2, ROWS, FEAT), BF),
            pltpu.VMEM((NB, NY - 1, 2, ROWS, FEAT), BF),
            pltpu.VMEM((NB, 2, 2, ROWS, FEAT), BF),
            pltpu.VMEM((NB, NX, 2, 2, CHUNK, FEAT), BF),
            pltpu.VMEM((NZ, 2, TOK, FEAT), F32),
            pltpu.VMEM((NZ, 2, TOK, FEAT), BF),
            pltpu.VMEM((NZ, 2, TOK, FEAT), BF),
            pltpu.VMEM((2, TOK, FEAT), F32),
            pltpu.VMEM((NZ, TOP, TOK), F32),
            pltpu.VMEM((NZ, TOP, TOK), F32),
            pltpu.VMEM((NZ, TOP, TOK), F32),
            pltpu.VMEM((TOP, TOK), F32),
            pltpu.VMEM((NT - 1, TOP, TOK), F32),
            pltpu.VMEM((NT, 8, FEAT), F32),
            pltpu.VMEM((NT, 8, FEAT), F32),
            pltpu.VMEM((NX, 8, FEAT), F32),
            pltpu.VMEM((NZ, 8, FEAT), F32),
            *dma(2 * (NT - 1), 32, NB * (NX - 1), NB * (NY - 1), NB),
            *dma(NB, NB * (NY - 1), NB * (NX - 1), 32, 2 * (NT - 1)),
            *dma(16, NT - 1, NT - 1, NX - 1, 16, NT - 1),
            pltpu.SemaphoreType.DMA((2 + 3 * NB,)),
        ],
        compiler_params=pltpu.CompilerParams(
            collective_id=0, has_side_effects=True, vmem_limit_bytes=60 * 2**20
        ),
        name="experts",
    )(normed, cotangent, meta, rmat, tri, gate_up, down_proj)


def shards(tokens, cotangent, gain, expert_ids, gate_probs, gate_up_weight, down_weight):
    t = lax.axis_index("tensor")
    values = tokens.astype(F32)
    inv_rms = lax.rsqrt(jnp.mean(values * values, axis=1, keepdims=True) + 1e-06)
    scaled = values * inv_rms
    normed = (scaled * gain[None, :]).astype(BF)
    probs_t = gate_probs.T
    high = lax.reduce_precision(probs_t, 8, 7)
    low = probs_t - high
    meta = jnp.concatenate(
        [
            jnp.concatenate([expert_ids.T.astype(F32), high], axis=0),
            jnp.concatenate([low, jnp.zeros_like(low)], axis=0),
        ],
        axis=1,
    ).astype(BF)
    summed, prob_sums, gain_sums, gate_up_grad, down_grad = experts(
        normed, cotangent, meta, gate_up_weight[0], down_weight[0]
    )
    mixed = (values + summed[0]).astype(BF)
    gain_side = summed[1] * gain[None, :]
    token_grad = (
        cotangent.astype(F32)
        + inv_rms * (gain_side - scaled * jnp.mean(gain_side * scaled, axis=1, keepdims=True))
    ).astype(BF)
    prob_grad = lax.dynamic_slice_in_dim(prob_sums, t * OWN, OWN, axis=1).T
    gain_grad = gain_sums[:, 0].reshape(-1) / gain
    return (mixed, token_grad, prob_grad, gain_grad, gate_up_grad[None], down_grad[None])


def solution(mesh):
    both = P(("expert", "tensor"), None)
    cube = P(("expert", "tensor"), None, None)
    in_specs = (both, both, P(), P("expert", None), P("expert", None), cube, cube)
    out_specs = (both, both, both, P(), cube, cube)
    return jax.shard_map(shards, mesh=mesh, in_specs=in_specs, out_specs=out_specs, check_vma=False)
```

time: 309 us -> 188 us (0.61)
  blocking collectives: 101 us -> 0 us
  Pallas kernels: 148 us -> 173 us
  matrix products: 15.2 us -> 0 us
  between operations: 14.3 us -> 0.68 us
  starting transfers between devices: 9.55 us -> 0 us
  other arithmetic: 11.9 us -> 7.98 us
    psum x1 -> x0, blocking collectives: 101 us -> none  [shards(): gain_grad = lax.psum(gain_part, ('expert', 'tensor')) / gain]
    pallas_call x2 -> x1, Pallas kernels: 148 us -> 173 us  [experts(): pl.pallas_call(experts_kernel, out_shape=(shape((2, OWN, features), F32),...]
    dot_general x7 -> x0, matrix products: 15.2 us -> none  [the longest x1 3.92 us: shards(): projected = jnp.dot(rows, gate_up, preferred_element_type=F32)]
    all_to_all x1 -> x0, starting transfers between devices: 9.32 us -> none  [shards(): lax.all_to_all(by_group, 'expert', split_axis=0, concat_axis=0, tiled=True)]
    another operation x3 -> x1, other arithmetic: 4.98 us -> 0.69 us  [the longest x1 3.2 us: shards(): summed = give_back(jnp.stack([block_out, input_grad]), codes, rmat)]
    unnamed x28 -> x10, local copies, waits for them, and re-layouts: 6.68 us -> 3.68 us
  transfers between devices with their start and end apart: 2 -> 0, of which waited for: 0 -> 0; matrix products, arithmetic and copies ran while one was open for 6% -> 0% of each run, Pallas kernels for 23% -> 0%
where the time goes in v2:
time: 188 us
  Pallas kernels  173 us (92%)
  other arithmetic  7.98 us (4%)
  local copies, waits for them, and re-layouts  5.88 us (3%)
    pallas_call x1, Pallas kernels, experts(): pl.pallas_call(experts_kernel, out_shape=(shape((2, OWN, features), F32),...  173 us

profile of v2, /device:TPU:1, one launch (start us, length us, event | category | flops | bytes accessed | tf_op | source)
XLA Modules:
  0.0 187.7 jit_solution(18347653391572825841)
XLA Ops:
  0.6 0.0 copy-start.3
  0.6 0.0 copy-start
  0.7 0.0 copy-start.2
  0.7 1.0 fusion.9
  1.7 0.7 fusion.14
  2.4 0.7 reduce-precision_convert_fusion
  3.1 0.6 fusion.12.meta_ref
  3.7 1.6 fusion.3.normed_ref
  5.2 173.1 %experts.1 = (f32[2,16,2048]{2,1,0:T(8,128)}, f32[8,128]{1,0:T(8,128)}, f32[8,8,256]{2,1,0:T(8,128)}, bf16[2048,384]{1,0:T(8,128)(2,1)}, bf16[192,2048]{1,0:T(8,128)(2,1)}) custom-call(bf16[16,2048]{1,0:T(8,128)(2,1)} %fusion.3.normed_ref, bf16[16,2048]{1,0:T(8,128)(2,1)} %cot_ref.1, bf16[16,256]{1,0:T(8,128)(2,1)} %fusion.12.meta_ref, ...), custom_call_target="tpu_custom_call" | custom-call | tf_op jit(solution)/shard_map/experts/pallas_call | solution.py:475
  178.4 1.4 dynamic-slice_bitcast_fusion
  179.7 0.0 copy-done.3
  179.7 0.0 copy-done
  179.7 1.1 fusion.4
  180.8 0.0 copy-done.2
  180.8 1.7 fusion.8
  182.6 0.8 slice.11
  183.4 0.6 div.11
  184.0 0.0 copy-start.1
  184.0 2.8 %copy.17 = bf16[1,2048,384]{2,1,0:T(8,128)(2,1)} copy(bf16[1,2048,384]{2,1,0:T(8,128)(2,1)} %bitcast.21) | data formatting | bytes 3145728
  186.8 0.0 copy-done.1
  186.8 0.9 copy.18
  (2 shorter events, 0.0 us)
Async XLA Ops:
  0.6 179.1 %copy-start.3 = (f32[2048]{0:T(1024)S(1)}, f32[2048]{0:T(1024)}, u32[]{:S(2)}) copy-start(f32[2048]{0:T(1024)} %param.11) | copy-start | bytes 24580
  0.6 179.1 %copy-start = (bf16[16,2048]{1,0:T(8,128)(2,1)S(1)}, bf16[16,2048]{1,0:T(8,128)(2,1)}, u32[]{:S(2)}) copy-start(bf16[16,2048]{1,0:T(8,128)(2,1)} %param.9) | copy-start | bytes 196612
  0.7 180.2 %copy-start.2 = (bf16[16,2048]{1,0:T(8,128)(2,1)S(1)}, bf16[16,2048]{1,0:T(8,128)(2,1)}, u32[]{:S(2)}) copy-start(bf16[16,2048]{1,0:T(8,128)(2,1)} %cot_ref.1) | copy-start | bytes 196612
  184.0 2.8 %copy-start.1 = (bf16[192,2048]{1,0:T(8,128)(2,1)S(1)}, bf16[192,2048]{1,0:T(8,128)(2,1)}, u32[]{:S(2)}) copy-start(bf16[192,2048]{1,0:T(8,128)(2,1)} %get-tuple-element.15) | copy-start | bytes 2359300

commit v3 on v2

--- a/solution.py
+++ b/solution.py
@@ -109,14 +109,14 @@
     for stay in stays:
         stay.wait()
 
-    pieces = (pl.ds(0, TOK), pl.ds(TOK, TOK + OWN))
+    pieces = (pl.ds(0, 96), pl.ds(96, 96), pl.ds(192, 80))
 
     def hop(step, way, p):
         sign = -1 if way == 0 else 1
         src, dst = SLOT_OF[sign * (step - 1)], SLOT_OF[sign * step]
         return go(
             zbuf.at[src, pieces[p], :], zbuf.at[dst, pieces[p], :], z_send, z_recv,
-            (way * 8 + step - 1) * 2 + p, right if way == 0 else left,
+            (way * 8 + step - 1) * len(pieces) + p, right if way == 0 else left,
         )
 
     def named_experts():
@@ -326,36 +326,43 @@
 
     ring = {}
 
-    def back_hop(step, way):
-        n = way * 8 + step
-        slot = SLOT_OF[8 - step] if way == 0 else SLOT_OF[-(7 - step)]
-        device = right if way == 0 else left
+    def back_hop(step):
+        ways = (0, 1) if step < 7 else (0,)
+        device = (right, left)
+        slot = (SLOT_OF[8 - step], SLOT_OF[-(7 - step)])
         for arr in range(2):
-            value = dense[slot, arr]
+            for part in range(2):
+                some = pl.ds(part * (TOK // 2), TOK // 2)
+                for way in ways:
+                    n = way * 8 + step
+                    value = dense[slot[way], arr, some, :]
+                    if step > 0:
+                        ring[way, step - 1, arr, part].wait_recv()
+                        value = value + ring_in[n - 1, arr, some, :].astype(F32)
+                    ring_out[n, arr, some, :] = value.astype(BF)
+                    ring[way, step, arr, part] = go(
+                        ring_out.at[n, arr, some, :], ring_in.at[n, arr, some, :], z2_send, z2_recv,
+                        4 * n + 2 * arr + part, device[way],
+                    )
+        for way in ways:
+            n = way * 8 + step
+            value = pdense[slot[way]]
             if step > 0:
-                ring[way, step - 1, arr].wait_recv()
-                value = value + ring_in[n - 1, arr].astype(F32)
-            ring_out[n, arr] = value.astype(BF)
-            ring[way, step, arr] = go(
-                ring_out.at[n, arr], ring_in.at[n, arr], z2_send, z2_recv, 2 * n + arr, device
-            )
-        value = pdense[slot]
-        if step > 0:
-            ring[way, step - 1, 2].wait_recv()
-            ring[way, step - 1, 3].wait_recv()
-            value = value + pring_in[n - 1]
-        pring_out[n] = value
-        ring[way, step, 2] = go(pring_out.at[n], pring_in.at[n], p_send, p_recv, n, device)
-        origin = lax.rem(z - step + NZ, NZ) if way == 0 else lax.rem(z + step, NZ)
-        ring[way, step, 3] = go(gz.at[origin], gz.at[origin], g3_send, g3_recv, n, device)
+                ring[way, step - 1, "prob"].wait_recv()
+                ring[way, step - 1, "gain"].wait_recv()
+                value = value + pring_in[n - 1]
+            pring_out[n] = value
+            ring[way, step, "prob"] = go(pring_out.at[n], pring_in.at[n], p_send, p_recv, n, device[way])
+            origin = lax.rem(z - step + NZ, NZ) if way == 0 else lax.rem(z + step, NZ)
+            ring[way, step, "gain"] = go(gz.at[origin], gz.at[origin], g3_send, g3_recv, n, device[way])
 
     flying = {}
-    for p in range(2):
+    for p in range(len(pieces)):
         for way in range(2):
             flying[way, p] = hop(1, way, p)
     xdone, ydone, cdone, back = {}, {}, {}, {}
     for step in range(1, 9):
-        for p in range(2):
+        for p in range(len(pieces)):
             for way in range(2):
                 last = 8 if way == 0 else 7
                 if step > last:
@@ -363,13 +370,13 @@
                 flying[way, p].wait_recv()
                 if step < last:
                     flying[way, p] = hop(step + 1, way, p)
+        b = step // 2 - 1
         if step % 2 == 0:
-            b = step // 2 - 1
             xdone[b] = stage_x(b)
-            if b >= 1:
-                ydone[b - 1] = stage_y(b - 1, xdone[b - 1])
             if b >= 2:
                 cdone[b - 2] = stage_c(b - 2, ydone[b - 2])
+        elif b >= 0:
+            ydone[b] = stage_y(b, xdone[b])
     ydone[3] = stage_y(3, xdone[3])
     back[0] = compute(0, cdone[0])
     cdone[2] = stage_c(2, ydone[2])
@@ -378,16 +385,16 @@
     cdone[3] = stage_c(3, ydone[3])
     back[3] = compute(3, cdone[3])
 
-    ysent = {}
-    for b in (3, 2, 1, 0):
-        ysent[b] = back_y(b, back[b])
+    ysent, xsent = {3: back_y(3, back[3])}, {}
     weight_grads()
+    ysent[2] = back_y(2, back[2])
     gains = []
     for i, other in others():
         their = phi_of(other)
         gains.append(go(gsend.at[their], gone.at[i], g1_send, g1_recv, i - 1, (e, other)))
     gone[0] = gsend[phi]
-    xsent = back_x(3, ysent[3])
+    xsent[3] = back_x(3, ysent[3])
+    ysent[1] = back_y(1, back[1])
     for copy in gains:
         copy.wait_recv()
     gain_sum = gone[0]
@@ -398,22 +405,31 @@
     for i in range(1, NX):
         other = lax.rem(x + i, NX)
         gains.append(go(gx.at[x], gx.at[x], g2_send, g2_recv, i - 1, (z * NX + other, t)))
+    spread(3, xsent[3])
     for copy in gains:
         copy.wait_recv()
     gz[z] = gx[0] + gx[1] + gx[2] + gx[3]
-    for n, b in enumerate((3, 2, 1, 0)):
-        if n > 0:
-            xsent = back_x(b, ysent[b])
-        spread(b, xsent)
-        for step in (2 * n, 2 * n + 1):
-            back_hop(step, 0)
-            if step < 7:
-                back_hop(step, 1)
+    back_hop(0)
+    xsent[2] = back_x(2, ysent[2])
+    ysent[0] = back_y(0, back[0])
+    back_hop(1)
+    spread(2, xsent[2])
+    back_hop(2)
+    xsent[1] = back_x(1, ysent[1])
+    back_hop(3)
+    spread(1, xsent[1])
+    back_hop(4)
+    xsent[0] = back_x(0, ysent[0])
+    back_hop(5)
+    spread(0, xsent[0])
+    back_hop(6)
+    back_hop(7)
 
     finals = []
     for arr in range(2):
-        ring[0, 7, arr].wait_recv()
-        ring[1, 6, arr].wait_recv()
+        for part in range(2):
+            ring[0, 7, arr, part].wait_recv()
+            ring[1, 6, arr, part].wait_recv()
         total[arr] = dense[0, arr] + ring_in[7, arr].astype(F32) + ring_in[8 + 6, arr].astype(F32)
         for i, other in others():
             n = arr * (NT - 1) + i - 1
@@ -429,7 +445,7 @@
         stay.start()
         stays.append(stay)
     for way in range(2):
-        for kind in (2, 3):
+        for kind in ("prob", "gain"):
             ring[way, 7 - way, kind].wait_recv()
     ptotal[...] = pdense[0] + pring_in[7] + pring_in[8 + 6]
     gain_sum = gz[0]
@@ -510,8 +526,8 @@
             pltpu.VMEM((NT, 8, FEAT), F32),
             pltpu.VMEM((NX, 8, FEAT), F32),
             pltpu.VMEM((NZ, 8, FEAT), F32),
-            *dma(2 * (NT - 1), 32, NB * (NX - 1), NB * (NY - 1), NB),
-            *dma(NB, NB * (NY - 1), NB * (NX - 1), 32, 2 * (NT - 1)),
+            *dma(2 * (NT - 1), 48, NB * (NX - 1), NB * (NY - 1), NB),
+            *dma(NB, NB * (NY - 1), NB * (NX - 1), 64, 2 * (NT - 1)),
             *dma(16, NT - 1, NT - 1, NX - 1, 16, NT - 1),
             pltpu.SemaphoreType.DMA((2 + 3 * NB,)),
         ],

time: 188 us -> 158 us (0.84)
  Pallas kernels: 173 us -> 143 us
    pallas_call x1, Pallas kernels: 173 us -> 143 us  [experts(): pl.pallas_call(experts_kernel, out_shape=(shape((2, OWN, features), F32),...]
where the time goes in v3:
time: 158 us
  Pallas kernels  143 us (91%)
  other arithmetic  7.98 us (5%)
  local copies, waits for them, and re-layouts  5.88 us (4%)
    pallas_call x1, Pallas kernels, experts(): pl.pallas_call(experts_kernel, out_shape=(shape((2, OWN, features), F32),...  143 us
    unnamed x10, local copies, waits for them, and re-layouts  3.68 us

profile of v3, /device:TPU:1, one launch (start us, length us, event | category | flops | bytes accessed | tf_op | source)
XLA Modules:
  0.0 157.7 jit_solution(5981240528290073897)
XLA Ops:
  0.6 0.0 copy-start.3
  0.6 0.0 copy-start
  0.7 0.0 copy-start.2
  0.7 1.0 fusion.9
  1.7 0.7 fusion.14
  2.4 0.7 reduce-precision_convert_fusion
  3.1 0.6 fusion.12.meta_ref
  3.7 1.6 fusion.3.normed_ref
  5.2 143.1 %experts.1 = (f32[2,16,2048]{2,1,0:T(8,128)}, f32[8,128]{1,0:T(8,128)}, f32[8,8,256]{2,1,0:T(8,128)}, bf16[2048,384]{1,0:T(8,128)(2,1)}, bf16[192,2048]{1,0:T(8,128)(2,1)}) custom-call(bf16[16,2048]{1,0:T(8,128)(2,1)} %fusion.3.normed_ref, bf16[16,2048]{1,0:T(8,128)(2,1)} %cot_ref.1, bf16[16,256]{1,0:T(8,128)(2,1)} %fusion.12.meta_ref, ...), custom_call_target="tpu_custom_call" | custom-call | tf_op jit(solution)/shard_map/experts/pallas_call | solution.py:491
  148.4 1.4 dynamic-slice_bitcast_fusion
  149.7 0.0 copy-done.3
  149.7 0.0 copy-done
  149.7 1.1 fusion.4
  150.9 0.0 copy-done.2
  150.9 1.7 %fusion.8 = (bf16[16,2048]{1,0:T(8,128)(2,1)}, bf16[16,2048]{1,0:T(8,128)(2,1)}) fusion(bf16[16,2048]{1,0:T(8,128)(2,1)S(1)} %copy-done, bf16[16,2048]{1,0:T(8,128)(2,1)S(1)} %copy-done.2, f32[2,16,2048]{2,1,0:T(8,128)} %get-tuple-element.11, f32[16]{0:T(128)S(1)} %broadcast_multiply_fusion, f32[2048]{0:T(1024)S(1)} %copy-done.3, f32[16]{0:T(128)S(1)} %add_rsqrt_fusion), kind=kLoop, calls=%fused_computation.11 | loop fusion | flops 360448 | bytes 532608 | tf_op jit(solution)/shard_map/convert_element_type | solution.py:565
  152.6 0.8 slice.11
  153.4 0.6 div.11
  154.0 0.0 copy-start.1
  154.0 2.8 %copy.17 = bf16[1,2048,384]{2,1,0:T(8,128)(2,1)} copy(bf16[1,2048,384]{2,1,0:T(8,128)(2,1)} %bitcast.21) | data formatting | bytes 3145728
  156.8 0.0 copy-done.1
  156.8 0.9 copy.18
  (2 shorter events, 0.0 us)
Async XLA Ops:
  0.6 149.1 %copy-start.3 = (f32[2048]{0:T(1024)S(1)}, f32[2048]{0:T(1024)}, u32[]{:S(2)}) copy-start(f32[2048]{0:T(1024)} %param.11) | copy-start | bytes 24580
  0.6 149.1 %copy-start = (bf16[16,2048]{1,0:T(8,128)(2,1)S(1)}, bf16[16,2048]{1,0:T(8,128)(2,1)}, u32[]{:S(2)}) copy-start(bf16[16,2048]{1,0:T(8,128)(2,1)} %param.9) | copy-start | bytes 196612
  0.7 150.2 %copy-start.2 = (bf16[16,2048]{1,0:T(8,128)(2,1)S(1)}, bf16[16,2048]{1,0:T(8,128)(2,1)}, u32[]{:S(2)}) copy-start(bf16[16,2048]{1,0:T(8,128)(2,1)} %cot_ref.1) | copy-start | bytes 196612
  154.0 2.8 %copy-start.1 = (bf16[192,2048]{1,0:T(8,128)(2,1)S(1)}, bf16[192,2048]{1,0:T(8,128)(2,1)}, u32[]{:S(2)}) copy-start(bf16[192,2048]{1,0:T(8,128)(2,1)} %get-tuple-element.15) | copy-start | bytes 2359300

commit v4 on v3

--- a/solution.py
+++ b/solution.py
@@ -46,12 +46,13 @@
     peers += [(lax.rem(z + i, NZ) * NX + x, t) for i in (1, NZ - 1)]
     for peer in peers:
         pl.semaphore_signal(barrier, inc=1, device_id=peer, device_id_type=pl.DeviceIdType.MESH)
-    pl.semaphore_wait(barrier, len(peers))
+    return barrier, len(peers)
 
 
 def experts_kernel(
-    normed_ref, cot_ref, meta_ref, rmat_ref, tri_ref, up_ref, down_ref,
-    out_ref, prob_ref, gain_ref, up_grad_ref, down_grad_ref,
+    token_ref, cot_ref, weight_ref, ids_ref, probs_ref, rmat_ref, tri_ref, up_ref, down_ref,
+    mixed_ref, token_grad_ref, prob_ref, gain_out_ref, up_grad_ref, down_grad_ref,
+    normed_ref, out_ref, gain_ref, prob_tall,
     zbuf, xs, yb, select, routed, parts, hid, joined,
     cb, ys, yr, q, xb, dense, ring_out, ring_in, total,
     pdense, pring_out, pring_in, ptotal, pgot, gsend, gone, gx, gz,
@@ -64,8 +65,22 @@
     phi = c * NY + y
     half = y // 2
     width = hid.shape[1]
-    greet(e, t, z, x)
+    barrier, count = greet(e, t, z, x)
     started = []
+
+    def normalize():
+        values = token_ref[...].astype(F32)
+        inv_rms = lax.rsqrt(jnp.mean(values * values, axis=1, keepdims=True) + 1e-06)
+        return values, inv_rms, values * inv_rms
+
+    normed_ref[...] = (normalize()[2] * weight_ref[...]).astype(BF)
+    probs = jnp.transpose(probs_ref[...])
+    high = probs.astype(BF).astype(F32)
+    low = probs - high
+    ids = jnp.transpose(ids_ref[...].astype(F32))
+    zbuf[0, 2 * TOK :, :TOK] = jnp.concatenate([ids, high], axis=0).astype(BF)
+    zbuf[0, 2 * TOK :, TOK:] = jnp.concatenate([low, jnp.zeros_like(low)], axis=0).astype(BF)
+    pl.semaphore_wait(barrier, count)
 
     def feat(index):
         return pl.ds(pl.multiple_of(index * FEAT, FEAT), FEAT)
@@ -103,7 +118,6 @@
         stay = pltpu.make_async_copy(ref.at[:, feat(phi)], zbuf.at[0, row_at, :], local.at[arr])
         stay.start()
         stays.append(stay)
-    zbuf[0, 2 * TOK :, :] = meta_ref[...]
     for copy in arrivals:
         copy.wait_recv()
     for stay in stays:
@@ -241,7 +255,7 @@
             summed = lax.dot_general(
                 jnp.ones((8, 2 * width), F32), grad * up_ref[cols, :].astype(F32), ACROSS,
                 precision=lax.Precision.HIGHEST, preferred_element_type=F32,
-            )
+            ) / weight_ref[:, cols]
             gsend[2 * n] = summed[:, :FEAT]
             gsend[2 * n + 1] = summed[:, FEAT:]
 
@@ -462,7 +476,17 @@
     prob_sum = ptotal[...]
     for i in range(NT - 1):
         prob_sum = prob_sum + pgot[i]
-    prob_ref[...] = prob_sum
+    prob_tall[...] = jnp.transpose(prob_sum)
+    prob_ref[...] = prob_tall[block16(t, OWN), :]
+    for n in range(NT):
+        gain_out_ref[:, n * FEAT : (n + 1) * FEAT] = gain_ref[n, 0:1, :]
+    values, inv_rms, scaled = normalize()
+    mixed_ref[...] = (values + out_ref[0]).astype(BF)
+    side = out_ref[1] * weight_ref[...]
+    token_grad_ref[...] = (
+        cot_ref[...].astype(F32)
+        + inv_rms * (side - scaled * jnp.mean(side * scaled, axis=1, keepdims=True))
+    ).astype(BF)
     for copy in started:
         copy.wait_send()
 
@@ -483,7 +507,7 @@
     return jnp.asarray(rmat, F32), jnp.asarray(tri, BF)
 
 
-def experts(normed, cotangent, meta, gate_up, down_proj):
+def experts(tokens, cotangent, gain, expert_ids, gate_probs, gate_up, down_proj):
     features, hidden = NT * FEAT, down_proj.shape[0]
     rows = NB * ROWS
     shape = jax.ShapeDtypeStruct
@@ -491,15 +515,20 @@
     return pl.pallas_call(
         experts_kernel,
         out_shape=(
-            shape((2, OWN, features), F32),
-            shape((TOP, TOK), F32),
-            shape((NT, 8, FEAT), F32),
+            shape((OWN, features), BF),
+            shape((OWN, features), BF),
+            shape((OWN, TOP), F32),
+            shape((1, features), F32),
             shape((features, 2 * hidden), BF),
             shape((hidden, features), BF),
         ),
-        in_specs=[vmem()] * 7,
-        out_specs=tuple([vmem()] * 5),
+        in_specs=[vmem()] * 9,
+        out_specs=tuple([vmem()] * 6),
         scratch_shapes=[
+            pltpu.VMEM((OWN, features), BF),
+            pltpu.VMEM((2, OWN, features), F32),
+            pltpu.VMEM((NT, 8, FEAT), F32),
+            pltpu.VMEM((TOK, TOP), F32),
             pltpu.VMEM((NZ, 2 * TOK + OWN, FEAT), BF),
             pltpu.VMEM((NB, NX, 2, 2, CHUNK, FEAT), BF),
             pltpu.VMEM((NB, 2, 2, ROWS, FEAT), BF),
@@ -535,37 +564,14 @@
             collective_id=0, has_side_effects=True, vmem_limit_bytes=60 * 2**20
         ),
         name="experts",
-    )(normed, cotangent, meta, rmat, tri, gate_up, down_proj)
+    )(tokens, cotangent, gain, expert_ids, gate_probs, rmat, tri, gate_up, down_proj)
 
 
 def shards(tokens, cotangent, gain, expert_ids, gate_probs, gate_up_weight, down_weight):
-    t = lax.axis_index("tensor")
-    values = tokens.astype(F32)
-    inv_rms = lax.rsqrt(jnp.mean(values * values, axis=1, keepdims=True) + 1e-06)
-    scaled = values * inv_rms
-    normed = (scaled * gain[None, :]).astype(BF)
-    probs_t = gate_probs.T
-    high = lax.reduce_precision(probs_t, 8, 7)
-    low = probs_t - high
-    meta = jnp.concatenate(
-        [
-            jnp.concatenate([expert_ids.T.astype(F32), high], axis=0),
-            jnp.concatenate([low, jnp.zeros_like(low)], axis=0),
-        ],
-        axis=1,
-    ).astype(BF)
-    summed, prob_sums, gain_sums, gate_up_grad, down_grad = experts(
-        normed, cotangent, meta, gate_up_weight[0], down_weight[0]
+    mixed, token_grad, prob_grad, gain_grad, gate_up_grad, down_grad = experts(
+        tokens, cotangent, gain[None], expert_ids, gate_probs, gate_up_weight[0], down_weight[0]
     )
-    mixed = (values + summed[0]).astype(BF)
-    gain_side = summed[1] * gain[None, :]
-    token_grad = (
-        cotangent.astype(F32)
-        + inv_rms * (gain_side - scaled * jnp.mean(gain_side * scaled, axis=1, keepdims=True))
-    ).astype(BF)
-    prob_grad = lax.dynamic_slice_in_dim(prob_sums, t * OWN, OWN, axis=1).T
-    gain_grad = gain_sums[:, 0].reshape(-1) / gain
-    return (mixed, token_grad, prob_grad, gain_grad, gate_up_grad[None], down_grad[None])
+    return (mixed, token_grad, prob_grad, gain_grad[0], gate_up_grad[None], down_grad[None])
 
 
 def solution(mesh):

time: 158 us -> 156 us (0.987)
  other arithmetic: 7.98 us -> 0 us
  local copies, waits for them, and re-layouts: 5.88 us -> 12.1 us
    unnamed x10, local copies, waits for them, and re-layouts: 3.68 us -> 12.1 us
    convert_element_type x3 -> x0, other arithmetic: 3.95 us -> none  [the longest x1 1.7 us: shards(): token_grad = (cotangent.astype(F32) + inv_rms * (gain_side - scaled * jnp...]
    reduce_sum x2 -> x0, other arithmetic: 2.12 us -> none  [the longest x1 1.1 us: shards(): jnp.mean(gain_side * scaled, axis=1, keepdims=True)]
where the time goes in v4:
time: 156 us
  Pallas kernels  143 us (92%)
  local copies, waits for them, and re-layouts  12.1 us (8%)
    pallas_call x1, Pallas kernels, experts(): pl.pallas_call(experts_kernel, out_shape=(shape((OWN, features), BF), sha...  143 us
    unnamed x10, local copies, waits for them, and re-layouts  12.1 us

profile of v4, /device:TPU:1, one launch (start us, length us, event | category | flops | bytes accessed | tf_op | source)
XLA Modules:
  0.0 156.1 jit_solution(3388007713796898237)
XLA Ops:
  0.6 1.4 copy.15.ids_ref
  2.0 1.4 copy.16.probs_ref
  3.5 143.3 %experts.1 = (bf16[16,2048]{1,0:T(8,128)(2,1)}, bf16[16,2048]{1,0:T(8,128)(2,1)}, f32[16,8]{1,0:T(8,128)}, f32[1,2048]{1,0:T(1,128)}, bf16[2048,384]{1,0:T(8,128)(2,1)}, /*index=5*/bf16[192,2048]{1,0:T(8,128)(2,1)}) custom-call(bf16[16,2048]{1,0:T(8,128)(2,1)} %token_ref.1, bf16[16,2048]{1,0:T(8,128)(2,1)} %cot_ref.1, f32[1,2048]{1,0:T(1,128)} %bitcast.10, ...), custom_call_target="tpu_custom_call" | custom-call | tf_op jit(solution)/shard_map/experts/pallas_call | solution.py:515
  146.8 1.4 copy.17
  148.2 1.5 copy.23
  149.6 1.5 copy.24
  151.1 1.3 copy.25
  152.4 0.0 copy-start
  152.4 2.8 %copy.26 = bf16[1,2048,384]{2,1,0:T(8,128)(2,1)} copy(bf16[1,2048,384]{2,1,0:T(8,128)(2,1)} %bitcast.6) | data formatting | bytes 3145728
  155.2 0.0 copy-done
  155.2 0.9 copy.27
Async XLA Ops:
  152.4 2.8 %copy-start = (bf16[192,2048]{1,0:T(8,128)(2,1)S(1)}, bf16[192,2048]{1,0:T(8,128)(2,1)}, u32[]{:S(2)}) copy-start(bf16[192,2048]{1,0:T(8,128)(2,1)} %get-tuple-element.17) | copy-start | bytes 2359300

commit v5 on v4

--- a/solution.py
+++ b/solution.py
@@ -74,12 +74,12 @@
         return values, inv_rms, values * inv_rms
 
     normed_ref[...] = (normalize()[2] * weight_ref[...]).astype(BF)
-    probs = jnp.transpose(probs_ref[...])
+    probs = probs_ref[...]
     high = probs.astype(BF).astype(F32)
     low = probs - high
-    ids = jnp.transpose(ids_ref[...].astype(F32))
-    zbuf[0, 2 * TOK :, :TOK] = jnp.concatenate([ids, high], axis=0).astype(BF)
-    zbuf[0, 2 * TOK :, TOK:] = jnp.concatenate([low, jnp.zeros_like(low)], axis=0).astype(BF)
+    ids = ids_ref[...].astype(F32)
+    zbuf[0, :OWN, :TOK] = jnp.concatenate([ids, high], axis=0).astype(BF)
+    zbuf[0, :OWN, TOK:] = jnp.concatenate([low, jnp.zeros_like(low)], axis=0).astype(BF)
     pl.semaphore_wait(barrier, count)
 
     def feat(index):
@@ -109,7 +109,7 @@
     stays = []
     arrivals = []
     for arr, ref in enumerate((normed_ref, cot_ref)):
-        row_at = block16(arr * (TOK // OWN) + t, OWN)
+        row_at = block16(1 + arr * (TOK // OWN) + t, OWN)
         for i, other in others():
             n = arr * (NT - 1) + i - 1
             arrivals.append(
@@ -118,10 +118,6 @@
         stay = pltpu.make_async_copy(ref.at[:, feat(phi)], zbuf.at[0, row_at, :], local.at[arr])
         stay.start()
         stays.append(stay)
-    for copy in arrivals:
-        copy.wait_recv()
-    for stay in stays:
-        stay.wait()
 
     pieces = (pl.ds(0, 96), pl.ds(96, 96), pl.ds(192, 80))
 
@@ -137,11 +133,11 @@
         base = lax.convert_element_type(z * (2 * NX), F32)
         return base + lax.broadcasted_iota(jnp.int32, (8, TOK), 0).astype(F32)
 
-    def stage_x(b):
+    def build(b):
         named = named_experts()
         chosen, high, low = [], [], []
         for j in range(BATCH):
-            meta = zbuf[b * BATCH + j, 2 * TOK :, :].astype(F32)
+            meta = zbuf[b * BATCH + j, :OWN, :].astype(F32)
             got, hi, lo = jnp.zeros((8, TOK), F32), jnp.zeros((8, TOK), F32), jnp.zeros((8, TOK), F32)
             for k in range(TOP):
                 same = meta[k : k + 1, :TOK] == named
@@ -168,9 +164,11 @@
             select[b, 0, rows, :] = jnp.where(hit, 1.0, 0.0).astype(BF)
             select[b, 1, rows, :] = jnp.where(hit, codes[8 + f : 9 + f, :], 0.0).astype(BF)
             select[b, 2, rows, :] = jnp.where(hit, codes[16 + f : 17 + f, :], 0.0).astype(BF)
+
+    def stage_x(b):
         these = pl.ds(b * BATCH, BATCH)
-        normed = zbuf[these, 0:TOK, :].reshape(WIDE, FEAT)
-        cot = zbuf[these, TOK : 2 * TOK, :].reshape(WIDE, FEAT)
+        normed = zbuf[these, OWN : OWN + TOK, :].reshape(WIDE, FEAT)
+        cot = zbuf[these, OWN + TOK :, :].reshape(WIDE, FEAT)
         picked = jnp.dot(select[b, 0], normed, preferred_element_type=F32).astype(BF)
         grads = (
             jnp.dot(select[b, 1], cot, preferred_element_type=F32)
@@ -301,7 +299,7 @@
     def spread(b, earlier):
         copies, stay = earlier
         these = pl.ds(b * BATCH, BATCH)
-        cot = zbuf[these, TOK : 2 * TOK, :].reshape(WIDE, FEAT)
+        cot = zbuf[these, OWN + TOK :, :].reshape(WIDE, FEAT)
         cot_slots = jnp.dot(select[b, 0], cot, preferred_element_type=F32)
         for copy in copies:
             copy.wait_recv()
@@ -328,7 +326,7 @@
         )
         named = named_experts()
         for j in range(BATCH):
-            ids = zbuf[b * BATCH + j, 2 * TOK :, :TOK].astype(F32)
+            ids = zbuf[b * BATCH + j, :OWN, :TOK].astype(F32)
             mine = by_expert[:, j * TOK : (j + 1) * TOK]
             pdense[b * BATCH + j] = jnp.concatenate(
                 [
@@ -372,6 +370,10 @@
 
     flying = {}
     for p in range(len(pieces)):
+        if p < 2:
+            for copy in arrivals[p * (NT - 1) : (p + 1) * (NT - 1)]:
+                copy.wait_recv()
+            stays[p].wait()
         for way in range(2):
             flying[way, p] = hop(1, way, p)
     xdone, ydone, cdone, back = {}, {}, {}, {}
@@ -384,6 +386,8 @@
                 flying[way, p].wait_recv()
                 if step < last:
                     flying[way, p] = hop(step + 1, way, p)
+            if p == 0 and step % 2 == 0:
+                build(step // 2 - 1)
         b = step // 2 - 1
         if step % 2 == 0:
             xdone[b] = stage_x(b)
@@ -569,7 +573,7 @@
 
 def shards(tokens, cotangent, gain, expert_ids, gate_probs, gate_up_weight, down_weight):
     mixed, token_grad, prob_grad, gain_grad, gate_up_grad, down_grad = experts(
-        tokens, cotangent, gain[None], expert_ids, gate_probs, gate_up_weight[0], down_weight[0]
+        tokens, cotangent, gain[None], expert_ids.T, gate_probs.T, gate_up_weight[0], down_weight[0]
     )
     return (mixed, token_grad, prob_grad, gain_grad[0], gate_up_grad[None], down_grad[None])
 

time: 156 us -> 153 us (0.981)
  local copies, waits for them, and re-layouts: 12.1 us -> 9.26 us
    unnamed x10 -> x8, local copies, waits for them, and re-layouts: 12.1 us -> 9.26 us
where the time goes in v5:
time: 153 us; the launch traced here: 152 us
  Pallas kernels  143 us (93%)
  local copies, waits for them, and re-layouts  9.26 us (6%)
    pallas_call x1, Pallas kernels, experts(): pl.pallas_call(experts_kernel, out_shape=(shape((OWN, features), BF), sha...  143 us
    unnamed x8, local copies, waits for them, and re-layouts  9.26 us

profile of v5, /device:TPU:1, one launch (start us, length us, event | category | flops | bytes accessed | tf_op | source)
XLA Modules:
  0.0 152.5 jit_solution(61351601591316856)
XLA Ops:
  0.6 142.6 %experts.1 = (bf16[16,2048]{1,0:T(8,128)(2,1)}, bf16[16,2048]{1,0:T(8,128)(2,1)}, f32[16,8]{1,0:T(8,128)}, f32[1,2048]{1,0:T(1,128)}, bf16[2048,384]{1,0:T(8,128)(2,1)}, /*index=5*/bf16[192,2048]{1,0:T(8,128)(2,1)}) custom-call(bf16[16,2048]{1,0:T(8,128)(2,1)} %token_ref.1, bf16[16,2048]{1,0:T(8,128)(2,1)} %cot_ref.1, f32[1,2048]{1,0:T(1,128)} %bitcast.12, ...), custom_call_target="tpu_custom_call" | custom-call | tf_op jit(solution)/shard_map/experts/pallas_call | solution.py:519
  143.2 1.4 copy.15
  144.6 1.5 copy.21
  146.0 1.5 copy.22
  147.5 1.3 copy.23
  148.8 0.0 copy-start
  148.8 2.8 %copy.24 = bf16[1,2048,384]{2,1,0:T(8,128)(2,1)} copy(bf16[1,2048,384]{2,1,0:T(8,128)(2,1)} %bitcast.9) | data formatting | bytes 3145728
  151.6 0.0 copy-done
  151.6 0.9 copy.25
Async XLA Ops:
  148.8 2.8 %copy-start = (bf16[192,2048]{1,0:T(8,128)(2,1)S(1)}, bf16[192,2048]{1,0:T(8,128)(2,1)}, u32[]{:S(2)}) copy-start(bf16[192,2048]{1,0:T(8,128)(2,1)} %get-tuple-element.17) | copy-start | bytes 2359300

commit v6 on v5

--- a/solution.py
+++ b/solution.py
@@ -242,12 +242,15 @@
             ).astype(BF)
         return go(parts.at[:, where, core_half(1 - c)], cb.at[b], c2_send, c2_recv, b, (e, y * NC + 1 - c))
 
-    def weight_grads():
+    def down_grads(n):
+        cols = pl.ds(n * 2 * FEAT, 2 * FEAT)
+        down_grad_ref[:, cols] = lax.dot_general(
+            hid[...], routed[1, :, cols], OVER, preferred_element_type=F32
+        ).astype(BF)
+
+    def up_grads():
         for n in range(4):
             cols = pl.ds(n * 2 * FEAT, 2 * FEAT)
-            down_grad_ref[:, cols] = lax.dot_general(
-                hid[...], routed[1, :, cols], OVER, preferred_element_type=F32
-            ).astype(BF)
             grad = lax.dot_general(routed[0, :, cols], joined[...], OVER, preferred_element_type=F32)
             up_grad_ref[cols, :] = grad.astype(BF)
             summed = lax.dot_general(
@@ -404,7 +407,7 @@
     back[3] = compute(3, cdone[3])
 
     ysent, xsent = {3: back_y(3, back[3])}, {}
-    weight_grads()
+    up_grads()
     ysent[2] = back_y(2, back[2])
     gains = []
     for i, other in others():
@@ -431,16 +434,20 @@
     xsent[2] = back_x(2, ysent[2])
     ysent[0] = back_y(0, back[0])
     back_hop(1)
+    down_grads(0)
     spread(2, xsent[2])
     back_hop(2)
     xsent[1] = back_x(1, ysent[1])
     back_hop(3)
+    down_grads(1)
     spread(1, xsent[1])
     back_hop(4)
     xsent[0] = back_x(0, ysent[0])
     back_hop(5)
+    down_grads(2)
     spread(0, xsent[0])
     back_hop(6)
+    down_grads(3)
     back_hop(7)
 
     finals = []

time: 153 us -> 153 us (level)
  no operation moved by 1% of the time
where the time goes in v6:
time: 153 us
  Pallas kernels  143 us (93%)
  local copies, waits for them, and re-layouts  9.26 us (6%)
    pallas_call x1, Pallas kernels, experts(): pl.pallas_call(experts_kernel, out_shape=(shape((OWN, features), BF), sha...  143 us
    unnamed x8, local copies, waits for them, and re-layouts  9.26 us

profile of v6, /device:TPU:1, one launch (start us, length us, event | category | flops | bytes accessed | tf_op | source)
XLA Modules:
  0.0 152.6 jit_solution(715480849116359361)
XLA Ops:
  0.6 142.7 %experts.1 = (bf16[16,2048]{1,0:T(8,128)(2,1)}, bf16[16,2048]{1,0:T(8,128)(2,1)}, f32[16,8]{1,0:T(8,128)}, f32[1,2048]{1,0:T(1,128)}, bf16[2048,384]{1,0:T(8,128)(2,1)}, /*index=5*/bf16[192,2048]{1,0:T(8,128)(2,1)}) custom-call(bf16[16,2048]{1,0:T(8,128)(2,1)} %token_ref.1, bf16[16,2048]{1,0:T(8,128)(2,1)} %cot_ref.1, f32[1,2048]{1,0:T(1,128)} %bitcast.12, ...), custom_call_target="tpu_custom_call" | custom-call | tf_op jit(solution)/shard_map/experts/pallas_call | solution.py:526
  143.3 1.4 copy.15
  144.7 1.5 copy.21
  146.1 1.5 copy.22
  147.6 1.3 copy.23
  148.9 0.0 copy-start
  148.9 2.8 %copy.24 = bf16[1,2048,384]{2,1,0:T(8,128)(2,1)} copy(bf16[1,2048,384]{2,1,0:T(8,128)(2,1)} %bitcast.9) | data formatting | bytes 3145728
  151.7 0.0 copy-done
  151.7 0.9 copy.25
Async XLA Ops:
  148.9 2.8 %copy-start = (bf16[192,2048]{1,0:T(8,128)(2,1)S(1)}, bf16[192,2048]{1,0:T(8,128)(2,1)}, u32[]{:S(2)}) copy-start(bf16[192,2048]{1,0:T(8,128)(2,1)} %get-tuple-element.17) | copy-start | bytes 2359300
